TPU v7x, 32 devices: a whole 2x2x4 slice. The times are simulated.
32 devices in a mesh: dp: 8 (over y, x, core), mp: 4 (over z).
Axes of the slice: x: 2, y: 2, z: 4, core: 2. Of those that a mesh axis runs over, the one named last changes fastest.
Arguments:
- tokens: bfloat16 [4096, 1536], P('dp'), may hold values from -40 to 40
- context: bfloat16 [512, 768], P('dp'), may hold values from -6 to 6
- frame_counts: int32 [4], replicated, may hold values from 512 to 1023, as said below
- text_counts: int32 [4], replicated, may hold values from 65 to 128, as said below
- w_qkv: bfloat16 [1536, 3, 1536], P('dp', None, 'mp'), may hold values from -0.15625 to 0.15625
- w_attn_out: bfloat16 [1536, 1536], P('mp', 'dp'), may hold values from -3 to 3
- w_cross_q: bfloat16 [1536, 1536], P('dp', 'mp'), may hold values from -0.15625 to 0.15625
- w_cross_kv: bfloat16 [768, 2, 1536], P('dp', None, 'mp'), may hold values from -0.21875 to 0.21875
- w_cross_out: bfloat16 [1536, 1536], P('mp', 'dp'), may hold values from -1 to 1
- w_in: bfloat16 [1536, 2, 6144], P('dp', None, 'mp'), may hold values from -0.15625 to 0.15625
- w_out: bfloat16 [6144, 1536], P('mp', 'dp'), may hold values from -0.078125 to 0.078125
- norm_gains: bfloat16 [3, 1536], P(None, 'dp'), may hold values from 0.5 to 1.5
- b_in: bfloat16 [2, 6144], P(None, ('mp', 'dp')), may hold values from -1.5 to 1.5
- b_out: bfloat16 [1536], P('dp'), may hold values from -1.5 to 1.5
- cotangent: bfloat16 [4096, 1536], P('dp'), may hold values from -6 to 6
Outputs:
- mixed: bfloat16 [4096, 1536], P('dp')
- grad_tokens: float32 [4096, 1536], P('dp')
- grad_qkv: float32 [1536, 3, 1536], P('dp', None, 'mp')
- grad_attn_out: float32 [1536, 1536], P('mp', 'dp')
- grad_cross_q: float32 [1536, 1536], P('dp', 'mp')
- grad_cross_kv: float32 [768, 2, 1536], P('dp', None, 'mp')
- grad_cross_out: float32 [1536, 1536], P('mp', 'dp')
- grad_in: float32 [1536, 2, 6144], P('dp', None, 'mp')
- grad_out: float32 [6144, 1536], P('mp', 'dp')
- grad_gains: float32 [3, 1536], P(None, 'dp')
- grad_b_in: float32 [2, 6144], P(None, ('mp', 'dp'))
- grad_b_out: float32 [1536], P('dp')
Inputs may be any that keep to these rules, and one draw needn't show every extreme that they name: Rows 1 to frame_counts[c] of clip c carry audio; one clip of every draw has 1023. `text_counts`: one clip of every draw has all 128 text tokens live.
All inputs are finite; a program needn't handle non-finite values.
Results may differ from a plain program's by a relative error of at most 0.018.
Values may be sent and summed in bfloat16 or wider, within the bound.
A program may use at most 192 MiB of HBM per device.

v0:
```python
import jax
import jax.numpy as jnp
from jax import lax
from jax.sharding import PartitionSpec as P

HD = 64


epsilon = 1e-05


def from_partner(block, axis, stride):
    count = lax.axis_size(axis)
    route = []
    for low in range(count):
        high = low | 1 << stride
        if high != low and high < count:
            route += [(low, high), (high, low)]
    return lax.ppermute(block, axis, route)


def layer_norm(values, gain_row):
    centered = values - jnp.mean(values, axis=-1, keepdims=True)
    spread = jnp.mean(centered * centered, axis=-1, keepdims=True)
    return centered * lax.rsqrt(spread + epsilon) * gain_row


def rotate(tensor, positions):
    quarter = tensor.shape[-1] // 4
    frequency = 10000.0 ** (-jnp.arange(quarter, dtype=jnp.float32) / quarter)
    angles = positions[:, None] * frequency[None, :]
    cosine = jnp.cos(angles)[:, None, :]
    sine_part = jnp.sin(angles)[:, None, :]
    first_part = tensor[..., :quarter]
    second = tensor[..., quarter : 2 * quarter]
    return jnp.concatenate(
        [
            first_part * cosine - second * sine_part,
            second * cosine + first_part * sine_part,
            tensor[..., 2 * quarter :],
        ],
        axis=-1,
    )


def gated_unit(both):
    gate = both[:, 0]
    return gate * jax.nn.sigmoid(gate) * both[:, 1]


def in_order(own_part, other_part, which_half):
    lower_first = jnp.concatenate([own_part, other_part], axis=0)
    upper_first = jnp.concatenate([other_part, own_part], axis=0)
    return jnp.where(which_half == 0, lower_first, upper_first)


def own_rows(whole, which_half, row_count):
    return lax.dynamic_slice_in_dim(whole, which_half * row_count, row_count, 0)


def partner_rows(whole, which_half, row_count):
    return lax.dynamic_slice_in_dim(whole, (1 - which_half) * row_count, row_count, 0)


def masked_scores(query_block, key_all, key_live):
    scale = query_block.shape[-1] ** (-0.5)
    raw_scores = (
        jnp.einsum("qhd,khd->hqk", query_block, key_all, preferred_element_type=jnp.float32) * scale
    )
    return jnp.where(key_live[None, None, :], raw_scores, -1e30)


def attend_forward(queries, key_all, value_all, key_live):
    row_count, head_count, head_size = queries.shape
    block_rows = min(512, row_count)
    blocks = queries.reshape(row_count // block_rows, block_rows, head_count, head_size)

    def per_block(query_block):
        scores = masked_scores(query_block, key_all, key_live)
        row_max = jnp.max(scores, axis=-1, keepdims=True)
        weights = jnp.exp(scores - row_max)
        row_total = jnp.sum(weights, axis=-1, keepdims=True)
        attn_probs = weights / row_total
        block_out = jnp.einsum(
            "hqk,khd->qhd",
            attn_probs.astype(jnp.bfloat16),
            value_all,
            preferred_element_type=jnp.float32,
        )
        return (block_out, row_max + jnp.log(row_total))

    outputs, log_sums = lax.map(per_block, blocks)
    return (outputs.reshape(row_count, head_count, head_size), log_sums)


def attend_backward(queries, key_all, value_all, key_live, log_sums, grad_out):
    row_count, head_count, head_size = queries.shape
    block_rows = min(512, row_count)
    block_shape = (row_count // block_rows, block_rows, head_count, head_size)
    scale = head_size ** (-0.5)

    def per_block(running, block_item):
        query_block, grad_block, lse_block = block_item
        attn_probs = jnp.exp(masked_scores(query_block, key_all, key_live) - lse_block)
        grad_probs = jnp.einsum(
            "qhd,khd->hqk", grad_block, value_all, preferred_element_type=jnp.float32
        )
        row_inner = jnp.sum(attn_probs * grad_probs, axis=-1, keepdims=True)
        grad_scores = (attn_probs * (grad_probs - row_inner)).astype(jnp.bfloat16)
        grad_query = (
            jnp.einsum("hqk,khd->qhd", grad_scores, key_all, preferred_element_type=jnp.float32)
            * scale
        )
        grad_key = (
            running[0]
            + jnp.einsum(
                "hqk,qhd->khd", grad_scores, query_block, preferred_element_type=jnp.float32
            )
            * scale
        )
        grad_value = running[1] + jnp.einsum(
            "hqk,qhd->khd",
            attn_probs.astype(jnp.bfloat16),
            grad_block,
            preferred_element_type=jnp.float32,
        )
        return ((grad_key, grad_value), grad_query)

    zero_keys = jnp.zeros(key_all.shape, jnp.float32)
    (grad_key, grad_value), grad_query = lax.scan(
        per_block,
        (zero_keys, zero_keys),
        (queries.reshape(block_shape), grad_out.reshape(block_shape), log_sums),
    )
    return (grad_query.reshape(row_count, head_count, head_size), grad_key, grad_value)


def branch_total(partial_sum):
    return lax.psum(partial_sum, "mp")


def grad_total(partial_sum):
    return lax.psum(partial_sum, "mp")


def body(
    tokens,
    context,
    frame_counts,
    text_counts,
    w_qkv,
    w_attn_out,
    w_cross_q,
    w_cross_kv,
    w_cross_out,
    w_in,
    w_out,
    norm_gains,
    b_in,
    b_out,
    cotangent,
):
    gathered = (
        lax.all_gather(w_qkv, "dp", axis=0, tiled=True),
        lax.all_gather(w_attn_out, "dp", axis=1, tiled=True),
        lax.all_gather(w_cross_q, "dp", axis=0, tiled=True),
        lax.all_gather(w_cross_kv, "dp", axis=0, tiled=True),
        lax.all_gather(w_cross_out, "dp", axis=1, tiled=True),
        lax.all_gather(w_in, "dp", axis=0, tiled=True),
        lax.all_gather(w_out, "dp", axis=1, tiled=True),
        lax.all_gather(norm_gains, "dp", axis=1, tiled=True),
        lax.all_gather(b_in, "dp", axis=1, tiled=True),
        lax.all_gather(b_out, "dp", axis=0, tiled=True),
    )
    (
        qkv_full,
        attn_out_full,
        cross_q_full,
        cross_kv_full,
        cross_out_full,
        in_full,
        out_full,
        gains_full,
        b_in_full,
        b_out_full,
    ) = gathered
    row_count, model_width = tokens.shape
    text_rows, text_width = context.shape
    head_cols = qkv_full.shape[2]
    unit_cols = in_full.shape[2]
    head_count = head_cols // HD
    device_row = lax.axis_index("dp")
    which_half = device_row % 2
    clip_index = device_row // 2
    frame_live = lax.dynamic_index_in_dim(frame_counts, clip_index, 0, keepdims=False)
    text_live = lax.dynamic_index_in_dim(text_counts, clip_index, 0, keepdims=False)
    positions = (which_half * row_count + jnp.arange(row_count)).astype(jnp.float32)
    key_live = jnp.arange(2 * row_count) <= frame_live
    token_live = jnp.arange(2 * text_rows) < text_live
    gain_rows = gains_full.astype(jnp.float32)
    tokens_f = tokens.astype(jnp.float32)
    grad_y_mine = cotangent.astype(jnp.float32)
    norm_one, pull_one = jax.vjp(layer_norm, tokens_f, gain_rows[0])
    h_one = norm_one.astype(jnp.bfloat16)
    qkv = jnp.dot(
        h_one, qkv_full.reshape(model_width, 3 * head_cols), preferred_element_type=jnp.float32
    ).reshape(row_count, 3, head_count, HD)
    queries = rotate(qkv[:, 0], positions).astype(jnp.bfloat16)
    own_keys = rotate(qkv[:, 1], positions).astype(jnp.bfloat16).reshape(row_count, head_cols)
    own_values = qkv[:, 2].astype(jnp.bfloat16).reshape(row_count, head_cols)
    own_text = jnp.dot(
        context,
        cross_kv_full.reshape(text_width, 2 * head_cols),
        preferred_element_type=jnp.float32,
    ).astype(jnp.bfloat16)
    other = from_partner((own_keys, own_values, own_text), "dp", 0)
    key_all = in_order(own_keys, other[0], which_half).reshape(2 * row_count, head_count, HD)
    value_all = in_order(own_values, other[1], which_half).reshape(2 * row_count, head_count, HD)
    text_all = in_order(own_text, other[2], which_half).reshape(2 * text_rows, 2, head_count, HD)
    text_keys = text_all[:, 0]
    text_values = text_all[:, 1]
    self_attn, self_lse = attend_forward(queries, key_all, value_all, key_live)
    self_out = self_attn.reshape(row_count, head_cols).astype(jnp.bfloat16)
    self_part = jnp.dot(self_out, attn_out_full, preferred_element_type=jnp.float32)
    x_one = tokens_f + branch_total(self_part)
    norm_two, pull_two = jax.vjp(layer_norm, x_one, gain_rows[1])
    h_two = norm_two.astype(jnp.bfloat16)
    cross_queries = (
        jnp.dot(h_two, cross_q_full, preferred_element_type=jnp.float32)
        .astype(jnp.bfloat16)
        .reshape(row_count, head_count, HD)
    )
    cross_attn, cross_lse = attend_forward(cross_queries, text_keys, text_values, token_live)
    cross_out = cross_attn.reshape(row_count, head_cols).astype(jnp.bfloat16)
    cross_part = jnp.dot(cross_out, cross_out_full, preferred_element_type=jnp.float32)
    x_two = x_one + branch_total(cross_part)
    norm_three, pull_three = jax.vjp(layer_norm, x_two, gain_rows[2])
    h_three = norm_three.astype(jnp.bfloat16)
    both = jnp.dot(
        h_three, in_full.reshape(model_width, 2 * unit_cols), preferred_element_type=jnp.float32
    ).reshape(row_count, 2, unit_cols) + b_in_full.astype(jnp.float32)
    hidden_f, pull_unit = jax.vjp(gated_unit, both)
    hidden = hidden_f.astype(jnp.bfloat16)
    down_part = jnp.dot(hidden, out_full, preferred_element_type=jnp.float32)
    mixed = (x_two + branch_total(down_part) + b_out_full.astype(jnp.float32)).astype(jnp.bfloat16)
    again = (
        lax.all_gather(w_qkv, "dp", axis=0, tiled=True),
        lax.all_gather(w_attn_out, "dp", axis=1, tiled=True),
        lax.all_gather(w_cross_q, "dp", axis=0, tiled=True),
        lax.all_gather(w_cross_out, "dp", axis=1, tiled=True),
        lax.all_gather(w_in, "dp", axis=0, tiled=True),
        lax.all_gather(w_out, "dp", axis=1, tiled=True),
    )
    qkv_back = again[0]
    attn_out_back = again[1]
    cross_q_back = again[2]
    cross_out_back = again[3]
    in_back = again[4]
    out_back = again[5]
    grad_y = cotangent.astype(jnp.float32)
    grad_out_w = jnp.dot(hidden.T, cotangent, preferred_element_type=jnp.float32)
    grad_b_out = jnp.sum(grad_y, axis=0)
    grad_hidden = jnp.dot(cotangent, out_back.T, preferred_element_type=jnp.float32)
    grad_both = pull_unit(grad_hidden)[0].astype(jnp.bfloat16).reshape(row_count, 2 * unit_cols)
    grad_b_in = jnp.sum(grad_both, axis=0, dtype=jnp.float32).reshape(2, unit_cols)
    grad_in_w = jnp.dot(h_three.T, grad_both, preferred_element_type=jnp.float32).reshape(
        model_width, 2, unit_cols
    )
    three_part = jnp.dot(
        grad_both, in_back.reshape(model_width, 2 * unit_cols).T, preferred_element_type=jnp.float32
    )
    grad_x_norm, grad_gain_three = pull_three(grad_total(three_part))
    grad_x_two = grad_y_mine + grad_x_norm
    grad_two_b = grad_x_two.astype(jnp.bfloat16)
    grad_cross_out_w = jnp.dot(cross_out.T, grad_two_b, preferred_element_type=jnp.float32)
    grad_cross = (
        jnp.dot(grad_two_b, cross_out_back.T, preferred_element_type=jnp.float32)
        .astype(jnp.bfloat16)
        .reshape(row_count, head_count, HD)
    )
    grad_cq, grad_text_key, grad_text_value = attend_backward(
        cross_queries, text_keys, text_values, token_live, cross_lse, grad_cross
    )
    grad_cq_b = grad_cq.reshape(row_count, head_cols).astype(jnp.bfloat16)
    grad_cross_q_w = jnp.dot(h_two.T, grad_cq_b, preferred_element_type=jnp.float32)
    grad_text = jnp.stack([grad_text_key, grad_text_value], axis=1).reshape(
        2 * text_rows, 2 * head_cols
    )
    two_part = jnp.dot(grad_cq_b, cross_q_back.T, preferred_element_type=jnp.float32)
    grad_x_norm, grad_gain_two = pull_two(grad_total(two_part))
    grad_x_one = grad_x_two + grad_x_norm
    grad_one_b = grad_x_one.astype(jnp.bfloat16)
    grad_attn_out_w = jnp.dot(self_out.T, grad_one_b, preferred_element_type=jnp.float32)
    grad_self = (
        jnp.dot(grad_one_b, attn_out_back.T, preferred_element_type=jnp.float32)
        .astype(jnp.bfloat16)
        .reshape(row_count, head_count, HD)
    )
    grad_query, grad_key_all, grad_value_all = attend_backward(
        queries, key_all, value_all, key_live, self_lse, grad_self
    )
    grad_key_flat = grad_key_all.reshape(2 * row_count, head_cols)
    grad_value_flat = grad_value_all.reshape(2 * row_count, head_cols)
    back = from_partner(
        (
            partner_rows(grad_key_flat, which_half, row_count),
            partner_rows(grad_value_flat, which_half, row_count),
            partner_rows(grad_text, which_half, text_rows),
        ),
        "dp",
        0,
    )
    grad_key_own = (own_rows(grad_key_flat, which_half, row_count) + back[0]).reshape(
        row_count, head_count, HD
    )
    grad_value_own = own_rows(grad_value_flat, which_half, row_count) + back[1]
    grad_text_own = (own_rows(grad_text, which_half, text_rows) + back[2]).astype(jnp.bfloat16)
    grad_query_raw = rotate(grad_query, -positions).reshape(row_count, head_cols)
    grad_key_raw = rotate(grad_key_own, -positions).reshape(row_count, head_cols)
    grad_qkv_b = (
        jnp.stack([grad_query_raw, grad_key_raw, grad_value_own], axis=1)
        .astype(jnp.bfloat16)
        .reshape(row_count, 3 * head_cols)
    )
    grad_qkv_w = jnp.dot(h_one.T, grad_qkv_b, preferred_element_type=jnp.float32).reshape(
        model_width, 3, head_cols
    )
    grad_cross_kv_w = jnp.dot(context.T, grad_text_own, preferred_element_type=jnp.float32).reshape(
        text_width, 2, head_cols
    )
    one_part = jnp.dot(
        grad_qkv_b,
        qkv_back.reshape(model_width, 3 * head_cols).T,
        preferred_element_type=jnp.float32,
    )
    grad_x_norm, grad_gain_one = pull_one(grad_total(one_part))
    grad_tokens = grad_x_one + grad_x_norm
    grad_gains = jnp.stack([grad_gain_one, grad_gain_two, grad_gain_three], axis=0)
    summed = (
        lax.psum_scatter(grad_qkv_w, "dp", scatter_dimension=0, tiled=True),
        lax.psum_scatter(grad_attn_out_w, "dp", scatter_dimension=1, tiled=True),
        lax.psum_scatter(grad_cross_q_w, "dp", scatter_dimension=0, tiled=True),
        lax.psum_scatter(grad_cross_kv_w, "dp", scatter_dimension=0, tiled=True),
        lax.psum_scatter(grad_cross_out_w, "dp", scatter_dimension=1, tiled=True),
        lax.psum_scatter(grad_in_w, "dp", scatter_dimension=0, tiled=True),
        lax.psum_scatter(grad_out_w, "dp", scatter_dimension=1, tiled=True),
        lax.psum_scatter(grad_gains, "dp", scatter_dimension=1, tiled=True),
        lax.psum_scatter(grad_b_in, "dp", scatter_dimension=1, tiled=True),
        lax.psum_scatter(grad_b_out, "dp", scatter_dimension=0, tiled=True),
    )
    return (
        mixed,
        grad_tokens,
        summed[0],
        summed[1],
        summed[2],
        summed[3],
        summed[4],
        summed[5],
        summed[6],
        summed[7],
        summed[8],
        summed[9],
    )


def solution(mesh):
    in_specs = (
        P("dp", None),
        P("dp", None),
        P(),
        P(),
        P("dp", None, "mp"),
        P("mp", "dp"),
        P("dp", "mp"),
        P("dp", None, "mp"),
        P("mp", "dp"),
        P("dp", None, "mp"),
        P("mp", "dp"),
        P(None, "dp"),
        P(None, ("mp", "dp")),
        P("dp"),
        P("dp", None),
    )
    out_specs = (
        P("dp", None),
        P("dp", None),
        P("dp", None, "mp"),
        P("mp", "dp"),
        P("dp", "mp"),
        P("dp", None, "mp"),
        P("mp", "dp"),
        P("dp", None, "mp"),
        P("mp", "dp"),
        P(None, "dp"),
        P(None, ("mp", "dp")),
        P("dp"),
    )
    return jax.shard_map(body, mesh=mesh, in_specs=in_specs, out_specs=out_specs, check_vma=False)
```

profile of v0, /device:TPU:0, one launch (start us, length us, event | category | flops | bytes accessed | tf_op | source)
XLA Modules:
  0.0 1617.1 jit_solution(996210380101947693)
XLA Ops:
  12.4 10.3 all-gather
  25.2 21.5 %all-gather.10.cloned.1.call-done = bf16[1536,3,384]{2,0,1:T(8,128)(2,1)} async-done(((bf16[192,3,384]{2,0,1:T(8,128)(2,1)}), bf16[1536,3,384]{2,0,1:T(8,128)(2,1)}) %all-gather.10.cloned.1.call-update) | async-done | bytes 3538960 | tf_op jit(solution)/shard_map/all_gather | solution.py:164
  46.7 6.1 copy.91
  52.8 4.2 fusion.30
  59.1 1.9 fusion.8
  61.1 3.0 fusion
  65.7 4.4 fusion.37
  70.1 2.5 all-gather.12.cloned.1.call-done
  72.6 4.0 fusion.75
  78.7 20.0 %all-gather.14.cloned.1.call-done = bf16[768,2,384]{2,1,0:T(2,128)(2,1)} async-done(((bf16[96,2,384]{2,1,0:T(2,128)(2,1)}), bf16[768,2,384]{2,1,0:T(2,128)(2,1)}) %all-gather.14.cloned.1.call-update) | async-done | bytes 1179664 | tf_op jit(solution)/shard_map/all_gather | solution.py:167
  102.6 120.0 %all-reduce.13.cloned.1.call-done = f32[512,1536]{1,0:T(8,128)} async-done(((f32[512,1536]{1,0:T(8,128)}), f32[512,1536]{1,0:T(8,128)}) %all-reduce.13.cloned.1.call-update) | async-done | bytes 3145744 | tf_op jit(solution)/shard_map/psum | solution.py:139
  222.6 2.7 fusion.72
  228.6 18.8 %all-gather.16.cloned.1.call-done = bf16[1536,384]{1,0:T(8,128)(2,1)} async-done(((bf16[192,384]{1,0:T(8,128)(2,1)}), bf16[1536,384]{1,0:T(8,128)(2,1)}) %all-gather.16.cloned.1.call-update) | async-done | bytes 1179664 | tf_op jit(solution)/shard_map/all_gather | solution.py:166
  247.4 2.6 convolution_convert_fusion.3
  254.1 19.1 %all-gather.18.cloned.1.call-done = bf16[384,1536]{0,1:T(8,128)(2,1)} async-done(((bf16[384,192]{0,1:T(8,128)(2,1)}), bf16[384,1536]{0,1:T(8,128)(2,1)}) %all-gather.18.cloned.1.call-update) | async-done | bytes 1179664 | tf_op jit(solution)/shard_map/all_gather | solution.py:168
  273.3 4.1 fusion.76
  277.4 2.4 copy.97
  280.7 9.1 all-gather.1
  291.7 106.9 %all-reduce.15.cloned.1.call-done = f32[512,1536]{1,0:T(8,128)} async-done(((f32[512,1536]{1,0:T(8,128)}), f32[512,1536]{1,0:T(8,128)}) %all-reduce.15.cloned.1.call-update) | async-done | bytes 3145744 | tf_op jit(solution)/shard_map/psum | solution.py:139
  398.6 2.3 fusion.71
  403.6 55.3 %all-gather.20.cloned.1.call-done = bf16[1536,2,1536]{2,0,1:T(8,128)(2,1)} async-done(((bf16[192,2,1536]{2,0,1:T(8,128)(2,1)}), bf16[1536,2,1536]{2,0,1:T(8,128)(2,1)}) %all-gather.20.cloned.1.call-update) | async-done | bytes 9437200 | tf_op jit(solution)/shard_map/all_gather | solution.py:169
  459.0 12.7 copy.98
  471.7 11.4 fusion.13
  483.1 16.7 %all-gather.22.cloned.1.call-done = bf16[1536,1536]{0,1:T(8,128)(2,1)} async-done(((bf16[1536,192]{0,1:T(8,128)(2,1)}), bf16[1536,1536]{0,1:T(8,128)(2,1)}) %all-gather.22.cloned.1.call-update) | async-done | bytes 4718608 | tf_op jit(solution)/shard_map/all_gather | solution.py:170
  499.8 9.4 multiply_bitcast_fusion
  512.0 9.4 convolution_bitcast_fusion
  522.7 120.0 %all-reduce.17.cloned.1.call-done = f32[512,1536]{1,0:T(8,128)} async-done(((f32[512,1536]{1,0:T(8,128)}), f32[512,1536]{1,0:T(8,128)}) %all-reduce.17.cloned.1.call-update) | async-done | bytes 3145744 | tf_op jit(solution)/shard_map/psum | solution.py:143
  642.7 4.5 multiply_reduce_fusion.1
  655.7 2.7 fusion.78
  659.1 7.1 fusion.77
  666.2 112.4 %all-reduce.19.cloned.1.call-done = f32[512,1536]{1,0:T(8,128)} async-done(((f32[512,1536]{1,0:T(8,128)}), f32[512,1536]{1,0:T(8,128)}) %all-reduce.19.cloned.1.call-update) | async-done | bytes 3145744 | tf_op jit(solution)/shard_map/psum | solution.py:143
  778.7 3.5 multiply_reduce_fusion.2
  788.5 6.0 multiply_reduce_fusion
  794.6 5.6 multiply_convert_fusion
  800.2 4.0 convolution_multiply_fusion
  805.3 2.7 fusion.4
  809.7 5.3 fusion.35
  820.6 6.0 convolution_bitcast_fusion.1
  829.2 4.9 copy.110
  837.6 5.4 copy.109
  843.1 206.0 %all-reduce.23.cloned.1.call-done = (f32[512,1536]{1,0:T(8,128)}, f32[512,1536]{1,0:T(8,128)}) async-done(((f32[512,1536]{1,0:T(8,128)}, f32[512,1536]{1,0:T(8,128)}), (f32[512,1536]{1,0:T(8,128)}, f32[512,1536]{1,0:T(8,128)})) %all-reduce.23.cloned.1.call-update) | async-done | bytes 6291472 | tf_op jit(solution)/shard_map/psum | solution.py:139
  1049.1 2.7 fusion.21
  1051.9 2.9 fusion.19
  1056.2 11.3 fusion.25
  1067.5 4.0 fusion.80
  1071.6 3.9 fusion.79
  1075.6 4.5 fusion.42
  1080.2 8.2 fusion.81
  1088.7 2.4 maximum_convert_fusion
  1091.1 2.4 copy.105
  1093.4 7.5 fusion.32
  1103.1 13.3 all-reduce.2
  1119.3 32.9 %all-reduce.21.cloned.1.call-done = f32[768,2,384]{2,1,0:T(2,128)} async-done(((f32[768,2,384]{2,1,0:T(2,128)}), f32[768,2,384]{2,1,0:T(2,128)}) %all-reduce.21.cloned.1.call-update) | async-done | bytes 2359312
  1153.9 12.4 all-reduce.4
  1167.0 4.0 add_convert_fusion.1
  1171.8 2.7 add_add_fusion.3
  1174.5 15.4 reduce-scatter.25.cloned.1.call-done
  1191.5 128.5 %reduce-scatter.21.cloned.1.call-done = f32[192,2,1536]{2,0,1:T(8,128)} async-done(((f32[1536,2,1536]{2,0,1:T(8,128)}), f32[192,2,1536]{2,0,1:T(8,128)}) %reduce-scatter.21.cloned.1.call-update) | async-done | bytes 2359312 | tf_op jit(solution)/shard_map/reduce_scatter | solution.py:345
  1320.0 4.9 copy.112
  1324.9 41.7 %reduce-scatter.19.cloned.1.call-done = f32[384,192]{0,1:T(8,128)} async-done(((f32[384,1536]{0,1:T(8,128)}), f32[384,192]{0,1:T(8,128)}) %reduce-scatter.19.cloned.1.call-update) | async-done | bytes 294928 | tf_op jit(solution)/shard_map/reduce_scatter | solution.py:344
  1366.6 46.3 %reduce-scatter.17.cloned.1.call-done = f32[192,384]{1,0:T(8,128)} async-done(((f32[1536,384]{1,0:T(8,128)}), f32[192,384]{1,0:T(8,128)}) %reduce-scatter.17.cloned.1.call-update) | async-done | bytes 294928 | tf_op jit(solution)/shard_map/reduce_scatter | solution.py:342
  1412.9 46.8 %reduce-scatter.15.cloned.1.call-done = f32[384,192]{0,1:T(8,128)} async-done(((f32[384,1536]{0,1:T(8,128)}), f32[384,192]{0,1:T(8,128)}) %reduce-scatter.15.cloned.1.call-update) | async-done | bytes 294928 | tf_op jit(solution)/shard_map/reduce_scatter | solution.py:341
  1459.7 80.5 %reduce-scatter.23.cloned.1.call-done = f32[1536,192]{0,1:T(8,128)} async-done(((f32[1536,1536]{0,1:T(8,128)}), f32[1536,192]{0,1:T(8,128)}) %reduce-scatter.23.cloned.1.call-update) | async-done | bytes 1179664 | tf_op jit(solution)/shard_map/reduce_scatter | solution.py:346
  1540.2 69.6 %reduce-scatter.13.cloned.1.call-done = f32[192,3,384]{2,0,1:T(8,128)} async-done(((f32[1536,3,384]{2,0,1:T(8,128)}), f32[192,3,384]{2,0,1:T(8,128)}) %reduce-scatter.13.cloned.1.call-update) | async-done | bytes 884752 | tf_op jit(solution)/shard_map/reduce_scatter | solution.py:340
  (343 shorter events, 73.1 us)
Async XLA Ops:
  7.2 93.0 %copy-start = (bf16[64,768]{1,0:T(8,128)(2,1)S(1)}, bf16[64,768]{1,0:T(8,128)(2,1)}, u32[]{:S(2)}) copy-start(bf16[64,768]{1,0:T(8,128)(2,1)} %param.16) | copy-start | bytes 294916
  7.2 5.2 copy-start.89
  7.2 15.7 copy-start.93
  7.2 39.4 %all-gather.10.cloned.1.call-start = ((), (), s32[]{:S(2)}) async-start(), calls=%async_computation.8 | async-start | bytes 3981312 | tf_op jit(solution)/shard_map/all_gather | solution.py:164
  8.0 64.7 %all-gather.12.cloned.1.call-start = ((), (), s32[]{:S(2)}) async-start(), calls=%async_computation.9 | async-start | bytes 1327104 | tf_op jit(solution)/shard_map/all_gather | solution.py:165
  8.7 90.0 %all-gather.14.cloned.1.call-start = ((), (), s32[]{:S(2)}) async-start(), calls=%async_computation.11 | async-start | bytes 1327104 | tf_op jit(solution)/shard_map/all_gather | solution.py:167
  9.4 213.2 %all-reduce.13.cloned.1.call-start = ((), (), s32[]{:S(2)}) async-start(), calls=%async_computation.10 | async-start | bytes 6291456 | tf_op jit(solution)/shard_map/psum | solution.py:139
  11.3 41.5 %copy-start.63 = (f32[512]{0:T(512)}, f32[512]{0:T(512)S(1)}, u32[]{:S(2)}) copy-start(f32[512]{0:T(512)S(1)} %broadcast_multiply_fusion.2) | copy-start | bytes 6148
  11.8 40.9 %copy-start.85 = (f32[512]{0:T(512)}, f32[512]{0:T(512)S(1)}, u32[]{:S(2)}) copy-start(f32[512]{0:T(512)S(1)} %fusion.50) | copy-start | bytes 6148
  22.9 29.9 %copy-start.51 = (f32[1536]{0:T(1024)}, f32[1536]{0:T(1024)S(1)}, u32[]{:S(2)}) copy-start(f32[1536]{0:T(1024)S(1)} %get-tuple-element.170) | copy-start | bytes 18436
  22.9 203.5 %copy-start.47 = (f32[1536]{0:T(1024)}, f32[1536]{0:T(1024)S(1)}, u32[]{:S(2)}) copy-start(f32[1536]{0:T(1024)S(1)} %get-tuple-element.169) | copy-start | bytes 18436
  22.9 448.8 %copy-start.53 = (f32[1536]{0:T(1024)}, f32[1536]{0:T(1024)S(1)}, u32[]{:S(2)}) copy-start(f32[1536]{0:T(1024)S(1)} %get-tuple-element.168) | copy-start | bytes 18436
  24.2 39.9 %copy-start.87 = (pred[1024]{0:T(1024)(128)(4,1)}, pred[1024]{0:T(1024)(128)(4,1)S(1)}, u32[]{:S(2)}) copy-start(pred[1024]{0:T(1024)(128)(4,1)S(1)} %iota_compare_fusion) | copy-start | bytes 3076
  57.3 1.8 collective-permute-start.1
  57.6 6.5 collective-permute-start
  58.1 6.1 copy-start.35
  64.1 6.0 copy-start.58
  64.1 6.0 copy-start.44
  70.1 6.5 copy-start.27
  72.6 5.4 copy-start.94
  76.7 170.8 %all-gather.16.cloned.1.call-start = ((), (), s32[]{:S(2)}) async-start(), calls=%async_computation.12 | async-start | bytes 1327104 | tf_op jit(solution)/shard_map/all_gather | solution.py:166
  77.2 196.0 %all-gather.18.cloned.1.call-start = ((), (), s32[]{:S(2)}) async-start(), calls=%async_computation.13 | async-start | bytes 1327104 | tf_op jit(solution)/shard_map/all_gather | solution.py:168
  77.8 320.8 %all-reduce.15.cloned.1.call-start = ((), (), s32[]{:S(2)}) async-start(), calls=%async_computation.14 | async-start | bytes 6291456 | tf_op jit(solution)/shard_map/psum | solution.py:139
  100.5 1.6 collective-permute-start.2
  228.6 22.1 %copy-start.91 = (pred[128]{0:T(512)(128)(4,1)S(1)}, pred[128]{0:T(512)(128)(4,1)}, u32[]{:S(2)}) copy-start(pred[128]{0:T(512)(128)(4,1)} %iota_compare_fusion.1) | copy-start | bytes 388
  277.4 181.6 %all-gather.20.cloned.1.call-start = ((), (), s32[]{:S(2)}) async-start(), calls=%async_computation.15 | async-start | bytes 10616832 | tf_op jit(solution)/shard_map/all_gather | solution.py:169
  279.9 219.9 %all-gather.22.cloned.1.call-start = ((), (), s32[]{:S(2)}) async-start(), calls=%async_computation.16 | async-start | bytes 5308416 | tf_op jit(solution)/shard_map/all_gather | solution.py:170
  280.6 362.1 %all-reduce.17.cloned.1.call-start = ((), (), s32[]{:S(2)}) async-start(), calls=%async_computation.17 | async-start | bytes 6291456 | tf_op jit(solution)/shard_map/psum | solution.py:143
  400.9 70.8 %copy-start.66 = (f32[512]{0:T(512)}, f32[512]{0:T(512)S(1)}, u32[]{:S(2)}) copy-start(f32[512]{0:T(512)S(1)} %broadcast_multiply_fusion) | copy-start | bytes 6148
  403.6 68.1 %copy-start.74 = (f32[512]{0:T(512)}, f32[512]{0:T(512)S(1)}, u32[]{:S(2)}) copy-start(f32[512]{0:T(512)S(1)} %fusion.52) | copy-start | bytes 6148
  521.4 257.2 %all-reduce.19.cloned.1.call-start = ((), (), s32[]{:S(2)}) async-start(), calls=%async_computation.18 | async-start | bytes 6291456 | tf_op jit(solution)/shard_map/psum | solution.py:143
  658.4 390.7 %all-reduce.23.cloned.1.call-start = ((), (), s32[]{:S(2)}) async-start(), calls=%async_computation.28 | async-start | bytes 12582912 | tf_op jit(solution)/shard_map/psum | solution.py:139
  659.1 119.5 %copy-start.48 = (f32[1536]{0:T(1024)S(1)}, f32[1536]{0:T(1024)}, u32[]{:S(2)}) copy-start(f32[1536]{0:T(1024)} %copy-done.47) | copy-start | bytes 18436
  659.1 119.5 %copy-start.62 = (f32[512]{0:T(512)S(1)}, f32[512]{0:T(512)}, u32[]{:S(2)}) copy-start(f32[512]{0:T(512)} %copy-done.61) | copy-start | bytes 6148
  659.1 119.5 %copy-start.70 = (f32[512]{0:T(512)S(1)}, f32[512]{0:T(512)}, u32[]{:S(2)}) copy-start(f32[512]{0:T(512)} %copy-done.69) | copy-start | bytes 6148
  666.2 116.0 %copy-start.82 = (f32[512]{0:T(512)S(1)}, f32[512]{0:T(512)}, u32[]{:S(2)}) copy-start(f32[512]{0:T(512)} %copy-done.81) | copy-start | bytes 6148
  783.3 5.2 slice-start.2
  794.6 5.6 copy-start.39
  794.6 5.6 copy-start.42
  800.2 5.1 copy-start.46
  800.2 5.0 copy-start.88
  805.2 10.9 collective-permute-start.3
  809.2 10.0 collective-permute-start.4
  819.0 7.6 copy-start.30
  819.2 7.4 copy-start.31
  820.6 6.1 copy-start.32
  826.7 291.0 %reduce-scatter.27.cloned.1.call-start = ((), (), s32[]{:S(2)}) async-start(), calls=%async_computation.26 | async-start | bytes 884736
  829.1 6.5 collective-permute-start.5
  829.2 6.4 copy-start.71
  835.3 316.9 %all-reduce.21.cloned.1.call-start = ((), (), s32[]{:S(2)}) async-start(), calls=%async_computation.27 | async-start | bytes 4718592
  837.5 5.5 copy-start.72
  837.5 211.5 %copy-start.6 = (bf16[512,1536]{1,0:T(8,128)(2,1)S(1)}, bf16[512,1536]{1,0:T(8,128)(2,1)}, u32[]{:S(2)}) copy-start(bf16[512,1536]{1,0:T(8,128)(2,1)} %param.15) | copy-start | bytes 4718596
  837.5 211.5 %copy-start.52 = (f32[1536]{0:T(1024)S(1)}, f32[1536]{0:T(1024)}, u32[]{:S(2)}) copy-start(f32[1536]{0:T(1024)} %copy-done.51) | copy-start | bytes 18436
  837.6 211.5 %copy-start.64 = (f32[512]{0:T(512)S(1)}, f32[512]{0:T(512)}, u32[]{:S(2)}) copy-start(f32[512]{0:T(512)} %copy-done.63) | copy-start | bytes 6148
  843.0 208.8 %copy-start.80 = (f32[512]{0:T(512)S(1)}, f32[512]{0:T(512)}, u32[]{:S(2)}) copy-start(f32[512]{0:T(512)} %copy-done.79) | copy-start | bytes 6148
  843.0 208.8 %copy-start.86 = (f32[512]{0:T(512)S(1)}, f32[512]{0:T(512)}, u32[]{:S(2)}) copy-start(f32[512]{0:T(512)} %copy-done.85) | copy-start | bytes 6148
  843.0 347.0 %reduce-scatter.25.cloned.1.call-start = ((), (), s32[]{:S(2)}) async-start(), calls=%async_computation.25 | async-start | bytes 884736
  1056.1 263.9 %reduce-scatter.21.cloned.1.call-start = ((), (), s32[]{:S(2)}) async-start(), calls=%async_computation.23 | async-start | bytes 21233664 | tf_op jit(solution)/shard_map/reduce_scatter | solution.py:345
  1067.5 299.2 %reduce-scatter.19.cloned.1.call-start = ((), (), s32[]{:S(2)}) async-start(), calls=%async_computation.22 | async-start | bytes 2654208 | tf_op jit(solution)/shard_map/reduce_scatter | solution.py:344
  1071.6 341.4 %reduce-scatter.17.cloned.1.call-start = ((), (), s32[]{:S(2)}) async-start(), calls=%async_computation.21 | async-start | bytes 2654208 | tf_op jit(solution)/shard_map/reduce_scatter | solution.py:342
  1075.5 384.2 %reduce-scatter.15.cloned.1.call-start = ((), (), s32[]{:S(2)}) async-start(), calls=%async_computation.20 | async-start | bytes 2654208 | tf_op jit(solution)/shard_map/reduce_scatter | solution.py:341
  1080.1 460.1 %reduce-scatter.23.cloned.1.call-start = ((), (), s32[]{:S(2)}) async-start(), calls=%async_computation.24 | async-start | bytes 10616832 | tf_op jit(solution)/shard_map/reduce_scatter | solution.py:346
  1088.3 521.5 %reduce-scatter.13.cloned.1.call-start = ((), (), s32[]{:S(2)}) async-start(), calls=%async_computation.19 | async-start | bytes 7962624 | tf_op jit(solution)/shard_map/reduce_scatter | solution.py:340
  1100.9 53.0 %copy-start.73 = (f32[1536]{0:T(1024)S(1)}, f32[1536]{0:T(1024)}, u32[]{:S(2)}) copy-start(f32[1536]{0:T(1024)} %get-tuple-element.188) | copy-start | bytes 18436
  (62 other events, 167.6 us)
Sparse Core Ops, SparseCore 0:
  10.0 36.6 all-gather.9
  48.5 24.0 all-gather.11
  74.5 24.1 all-gather.13
  101.5 121.0 all-reduce.12
  224.3 23.0 all-gather.15
  249.2 24.0 all-gather.17
  277.5 121.0 all-reduce.14
  401.1 57.8 all-gather.19
  460.9 38.9 all-gather.21
  521.5 121.0 all-reduce.16
  658.5 120.0 all-reduce.18
  826.8 222.2 all-reduce.22
  1052.2 33.9 reduce-scatter.26
  1089.3 62.8 all-reduce.20
  1155.5 34.3 reduce-scatter.24
  1193.9 126.0 reduce-scatter.20
  1324.1 42.4 reduce-scatter.18
  1370.4 42.4 reduce-scatter.16
  1417.2 42.4 reduce-scatter.14
  1463.7 76.4 reduce-scatter.22
  1544.3 65.4 reduce-scatter.12
where the time goes:
time: 1630 us; the launch traced here: 1620 us
  waiting for transfers between devices  1290 us (79%)
  matrix products  132 us (8%)
  local copies, waits for them, and re-layouts  77 us (5%)
  other arithmetic  55.6 us (3%)
  blocking collectives  45.1 us (3%)
  between operations  18.1 us (1%)
    psum x3, waiting for transfers between devices, branch_total(): return lax.psum(partial_sum, 'mp')  433 us
    psum x2, waiting for transfers between devices, grad_total(): return lax.psum(partial_sum, 'mp')  232 us
    reduce_scatter x1, waiting for transfers between devices, body(): lax.psum_scatter(grad_in_w, 'dp', scatter_dimension=0, tiled=True)  128 us
    reduce_scatter x1, waiting for transfers between devices, body(): lax.psum_scatter(grad_out_w, 'dp', scatter_dimension=1, tiled=True)  80.5 us
    reduce_scatter x1, waiting for transfers between devices, body(): lax.psum_scatter(grad_qkv_w, 'dp', scatter_dimension=0, tiled=True)  69.6 us
    all_gather x1, waiting for transfers between devices, body(): lax.all_gather(w_in, 'dp', axis=0, tiled=True)  55.3 us
    unnamed x24, waiting for transfers between devices  52.4 us
    reduce_scatter x1, waiting for transfers between devices, body(): lax.psum_scatter(grad_attn_out_w, 'dp', scatter_dimension=1, tiled=True)  46.8 us
  transfers between devices with their start and end apart: 27, of which 21 were waited for; matrix products, arithmetic and copies ran while one was open for 11% of the time, Pallas kernels for 0%

commit v1 on v0

--- a/solution.py
+++ b/solution.py
@@ -1,9 +1,364 @@
+import functools
+
 import jax
 import jax.numpy as jnp
 from jax import lax
+from jax.experimental import pallas as pl
+from jax.experimental.pallas import tpu as pltpu
 from jax.sharding import PartitionSpec as P
 
 HD = 64
+MESH = pl.DeviceIdType.MESH
+HBM = pl.BlockSpec(memory_space=pl.ANY)
+
+
+def greet(peers):
+    barrier = pltpu.get_barrier_semaphore()
+    for peer in peers:
+        pl.semaphore_signal(barrier, inc=1, device_id=peer, device_id_type=MESH)
+    pl.semaphore_wait(barrier, len(peers))
+
+
+def send(src, dst, send_sem, recv_sem, peer):
+    return pltpu.make_async_remote_copy(
+        src_ref=src,
+        dst_ref=dst,
+        send_sem=send_sem,
+        recv_sem=recv_sem,
+        device_id=peer,
+        device_id_type=MESH,
+    )
+
+
+def dp_peers():
+    d = lax.axis_index("dp")
+    m = lax.axis_index("mp")
+    return d, [(jnp.bitwise_xor(d, 1), m), (jnp.bitwise_xor(d, 2), m), (jnp.bitwise_xor(d, 4), m)]
+
+
+def gather_kernel(count, *refs):
+    ins, outs = refs[:count], refs[count : 2 * count]
+    send_sems, recv_sems, local_sems = refs[2 * count :]
+    d, (core, xn, yn) = dp_peers()
+    greet((core, xn, yn))
+    started = []
+    local = []
+
+    def go(a, k, block, rows, peer):
+        lo, size = rows
+        part = outs[a].at[block, pl.ds(lo, size)] if size else outs[a].at[block]
+        cp = send(part, part, send_sems.at[a, k], recv_sems.at[a, k], peer)
+        cp.start()
+        started.append(cp)
+
+    def own(a, k, peer):
+        cp = send(ins[a], outs[a].at[d], send_sems.at[a, k], recv_sems.at[a, k], peer)
+        cp.start()
+        started.append(cp)
+
+    def got(a, k, block, rows, peer):
+        lo, size = rows
+        part = outs[a].at[block, pl.ds(lo, size)] if size else outs[a].at[block]
+        send(part, part, send_sems.at[a, k], recv_sems.at[a, k], peer).wait_recv()
+
+    bx, by, bd = jnp.bitwise_xor(d, 2), jnp.bitwise_xor(d, 4), jnp.bitwise_xor(d, 6)
+    b1 = jnp.bitwise_xor(d, 1)
+    whole = (0, 0)
+    for a in range(count):
+        own(a, 0, xn)
+        own(a, 1, yn)
+        own(a, 2, core)
+        cp = pltpu.make_async_copy(ins[a], outs[a].at[d], local_sems.at[a])
+        cp.start()
+        local.append(cp)
+    for a in range(count):
+        half = ins[a].shape[0] // 2
+        top, bottom = (0, half), (half, half)
+        got(a, 0, bx, whole, xn)
+        go(a, 3, bx, top, yn)
+        go(a, 5, bx, whole, core)
+        got(a, 1, by, whole, yn)
+        go(a, 4, by, bottom, xn)
+        go(a, 6, by, whole, core)
+        got(a, 3, bd, top, yn)
+        go(a, 7, bd, top, core)
+        got(a, 4, bd, bottom, xn)
+        go(a, 8, bd, bottom, core)
+    for a in range(count):
+        half = ins[a].shape[0] // 2
+        top, bottom = (0, half), (half, half)
+        got(a, 2, b1, whole, core)
+        got(a, 5, jnp.bitwise_xor(bx, 1), whole, core)
+        got(a, 6, jnp.bitwise_xor(by, 1), whole, core)
+        got(a, 7, jnp.bitwise_xor(bd, 1), top, core)
+        got(a, 8, jnp.bitwise_xor(bd, 1), bottom, core)
+    for cp in started:
+        cp.wait_send()
+    for cp in local:
+        cp.wait()
+
+
+def gather_all(arrays, collective_id):
+    count = len(arrays)
+    outs = pl.pallas_call(
+        functools.partial(gather_kernel, count),
+        out_shape=[jax.ShapeDtypeStruct((8,) + a.shape, a.dtype) for a in arrays],
+        in_specs=[HBM] * count,
+        out_specs=[HBM] * count,
+        scratch_shapes=[
+            pltpu.SemaphoreType.DMA((count, 9)),
+            pltpu.SemaphoreType.DMA((count, 9)),
+            pltpu.SemaphoreType.DMA((count,)),
+        ],
+        compiler_params=pltpu.CompilerParams(collective_id=collective_id, has_side_effects=True),
+        name="gather_all",
+    )(*arrays)
+    return [o.reshape((-1,) + o.shape[2:]) for o in outs]
+
+
+CH = 32
+
+
+def line_kernel(n, x_ref, o_ref, own, got, res, load_sem, send_sems, recv_sems, back_send, back_recv):
+    d = lax.axis_index("dp")
+    z = lax.axis_index("mp")
+    rows = x_ref.shape[0]
+    half = rows // 2
+    chunks = half // CH
+    load = pltpu.make_async_copy(x_ref, own, load_sem)
+    load.start()
+    barrier = pltpu.get_barrier_semaphore()
+
+    @pl.when(z > 0)
+    def _():
+        pl.semaphore_signal(barrier, inc=1, device_id=(d, z - 1), device_id_type=MESH)
+
+    @pl.when(z < n - 1)
+    def _():
+        pl.semaphore_signal(barrier, inc=1, device_id=(d, z + 1), device_id_type=MESH)
+
+    @pl.when((z > 0) & (z < n - 1))
+    def _():
+        pl.semaphore_wait(barrier, 2)
+
+    @pl.when((z == 0) | (z == n - 1))
+    def _():
+        pl.semaphore_wait(barrier, 1)
+
+    load.wait()
+
+    def out_copy(f, c, nxt):
+        at = pl.ds(pl.multiple_of(f * half + c * CH, CH), CH)
+        return send(own.at[at], got.at[at], send_sems.at[f, c], recv_sems.at[f, c], (d, nxt))
+
+    def back_copy(f, c, prv):
+        at = pl.ds(pl.multiple_of(f * half + c * CH, CH), CH)
+        return send(res.at[at], res.at[at], back_send.at[f, c], back_recv.at[f, c], (d, prv))
+
+    def slot(s, carry):
+        for f in range(2):
+            p = z if f else n - 1 - z
+            nxt = z + 1 if f else z - 1
+            prv = z - 1 if f else z + 1
+            c = s - p
+
+            @pl.when((c >= 0) & (c < chunks))
+            def _():
+                at = pl.ds(pl.multiple_of(f * half + c * CH, CH), CH)
+
+                @pl.when(p > 0)
+                def _():
+                    out_copy(f, c, nxt).wait_recv()
+                    own[at] = (own[at].astype(jnp.float32) + got[at].astype(jnp.float32)).astype(
+                        jnp.bfloat16
+                    )
+
+                @pl.when(p < n - 1)
+                def _():
+                    out_copy(f, c, nxt).start()
+
+                @pl.when(p == n - 1)
+                def _():
+                    res[at] = own[at]
+                    back_copy(f, c, prv).start()
+
+            b = s - 2 * (n - 1) + p
+
+            @pl.when((b >= 0) & (b < chunks) & (p < n - 1))
+            def _():
+                back_copy(f, b, prv).wait_recv()
+
+                @pl.when(p > 0)
+                def _():
+                    back_copy(f, b, prv).start()
+
+        return carry
+
+    lax.fori_loop(0, chunks + 2 * (n - 1), slot, 0)
+
+    def drain(c, carry):
+        for f in range(2):
+            p = z if f else n - 1 - z
+            nxt = z + 1 if f else z - 1
+            prv = z - 1 if f else z + 1
+
+            @pl.when(p < n - 1)
+            def _():
+                out_copy(f, c, nxt).wait_send()
+
+            @pl.when(p > 0)
+            def _():
+                back_copy(f, c, prv).wait_send()
+
+        return carry
+
+    lax.fori_loop(0, chunks, drain, 0)
+    store = pltpu.make_async_copy(res, o_ref, load_sem)
+    store.start()
+    store.wait()
+
+
+def line_sum(x, n, collective_id):
+    shape = x.shape
+    chunks = shape[0] // 2 // CH
+    return pl.pallas_call(
+        functools.partial(line_kernel, n),
+        out_shape=jax.ShapeDtypeStruct(shape, x.dtype),
+        in_specs=[HBM],
+        out_specs=HBM,
+        scratch_shapes=[pltpu.VMEM(shape, x.dtype)] * 3
+        + [pltpu.SemaphoreType.DMA]
+        + [pltpu.SemaphoreType.DMA((2, chunks))] * 4,
+        compiler_params=pltpu.CompilerParams(
+            collective_id=collective_id, has_side_effects=True, vmem_limit_bytes=32 * 2**20
+        ),
+        name="line_sum",
+    )(x)
+
+
+def scatter_kernel(count, *refs):
+    ins, outs = refs[:count], refs[count : 2 * count]
+    rest = refs[2 * count :]
+    own, got, one, two, out_v = [rest[i * count : (i + 1) * count] for i in range(5)]
+    send_sems, recv_sems, local_sems = rest[5 * count :]
+    d, (core, xn, yn) = dp_peers()
+    c = lax.rem(d, 2)
+    x = lax.rem(d // 2, 2)
+    y = d // 4
+    greet((core, xn, yn))
+    copies = [{} for _ in range(count)]
+    loads, stores = [], []
+
+    def go(a, k, src, dst, peer):
+        cp = send(src, dst, send_sems.at[a, k], recv_sems.at[a, k], peer)
+        cp.start()
+        copies[a][k] = cp
+
+    for a in range(count):
+        go(a, 0, ins[a].at[:, 1 - c], got[a], core)
+        cp = pltpu.make_async_copy(ins[a].at[:, c], own[a], local_sems.at[a])
+        cp.start()
+        loads.append(cp)
+
+    def add_core(a):
+        loads[a].wait()
+        copies[a][0].wait_recv()
+        rows = own[a].shape[1]
+
+        def tile(i, carry):
+            j, t = i // (rows // 16), lax.rem(i, rows // 16)
+            at = pl.ds(pl.multiple_of(t * 16, 16), 16)
+            own[a][j, at] = (own[a][j, at].astype(jnp.float32) + got[a][j, at].astype(jnp.float32)).astype(
+                jnp.bfloat16
+            )
+            return carry
+
+        lax.fori_loop(0, 4 * (rows // 16), tile, 0)
+        half = rows // 2
+        top, bottom = pl.ds(0, half), pl.ds(half, half)
+        for b in range(2):
+            go(a, 1 + b, own[a].at[2 * b + 1 - x, top], one[a].at[0, b], xn)
+            go(a, 3 + b, own[a].at[2 * (1 - y) + b, bottom], one[a].at[1, b], yn)
+
+    def plus(a, at_block, lo, part):
+        half = own[a].shape[1] // 2
+
+        def tile(t, carry):
+            at = pl.ds(pl.multiple_of(lo + t * 16, 16), 16)
+            frm = pl.ds(pl.multiple_of(t * 16, 16), 16)
+            own[a][at_block, at] = (
+                own[a][at_block, at].astype(jnp.float32) + part[frm].astype(jnp.float32)
+            ).astype(jnp.bfloat16)
+            return carry
+
+        lax.fori_loop(0, half // 16, tile, 0)
+
+    def add_one(a):
+        half = own[a].shape[1] // 2
+        top, bottom = pl.ds(0, half), pl.ds(half, half)
+        for b in range(2):
+            copies[a][1 + b].wait_recv()
+            plus(a, 2 * b + x, 0, one[a].at[0, b])
+            copies[a][3 + b].wait_recv()
+            plus(a, 2 * y + b, half, one[a].at[1, b])
+        go(a, 5, own[a].at[2 * (1 - y) + x, top], two[a].at[0], yn)
+        go(a, 6, own[a].at[2 * y + 1 - x, bottom], two[a].at[1], xn)
+
+    def add_two(a):
+        half = own[a].shape[1] // 2
+        for part in range(2):
+            copies[a][5 + part].wait_recv()
+
+            def tile(t, carry, part=part):
+                at = pl.ds(pl.multiple_of(part * half + t * 16, 16), 16)
+                frm = pl.ds(pl.multiple_of(t * 16, 16), 16)
+                out_v[a][at] = own[a][2 * y + x, at].astype(jnp.float32) + two[a][part, frm].astype(jnp.float32)
+                return carry
+
+            lax.fori_loop(0, half // 16, tile, 0)
+        cp = pltpu.make_async_copy(out_v[a], outs[a], local_sems.at[a])
+        cp.start()
+        stores.append(cp)
+
+    for s in range(count + 2):
+        if s < count:
+            add_core(s)
+        if 0 <= s - 1 < count:
+            add_one(s - 1)
+        if 0 <= s - 2 < count:
+            add_two(s - 2)
+    for a in range(count):
+        for cp in copies[a].values():
+            cp.wait_send()
+    for cp in stores:
+        cp.wait()
+
+
+def scatter_all(arrays, collective_id):
+    count = len(arrays)
+    views = [a.reshape(4, 2, a.shape[0] // 8, a.shape[1]) for a in arrays]
+    sizes = [v.shape[2:] for v in views]
+    bf = jnp.bfloat16
+    return pl.pallas_call(
+        functools.partial(scatter_kernel, count),
+        out_shape=[jax.ShapeDtypeStruct(s, jnp.float32) for s in sizes],
+        in_specs=[HBM] * count,
+        out_specs=[HBM] * count,
+        scratch_shapes=[pltpu.VMEM((4,) + s, bf) for s in sizes]
+        + [pltpu.VMEM((4,) + s, bf) for s in sizes]
+        + [pltpu.VMEM((2, 2, s[0] // 2, s[1]), bf) for s in sizes]
+        + [pltpu.VMEM((2, s[0] // 2, s[1]), bf) for s in sizes]
+        + [pltpu.VMEM(s, jnp.float32) for s in sizes]
+        + [
+            pltpu.SemaphoreType.DMA((count, 7)),
+            pltpu.SemaphoreType.DMA((count, 7)),
+            pltpu.SemaphoreType.DMA((count,)),
+        ],
+        compiler_params=pltpu.CompilerParams(
+            collective_id=collective_id, has_side_effects=True, vmem_limit_bytes=60 * 2**20
+        ),
+        name="scatter_all",
+    )(*views)
 
 
 epsilon = 1e-05
@@ -141,6 +496,203 @@
 
 def grad_total(partial_sum):
     return lax.psum(partial_sum, "mp")
+
+
+def near_body(
+    tokens,
+    context,
+    frame_counts,
+    text_counts,
+    w_qkv,
+    w_attn_out,
+    w_cross_q,
+    w_cross_kv,
+    w_cross_out,
+    w_in,
+    w_out,
+    norm_gains,
+    b_in,
+    b_out,
+    cotangent,
+):
+    n = lax.axis_size("mp")
+    shard, _, head_cols = w_qkv.shape
+    unit_cols = w_in.shape[2]
+    bf = jnp.bfloat16
+    vec = jnp.concatenate([norm_gains, b_in, b_out[None]], axis=0)
+    vec = jnp.pad(vec, ((0, 32 - vec.shape[0]), (0, 256 - shard)))
+    vec_full, qkv_full, small_full, ckv_full, out_t, in_full = gather_all(
+        [
+            vec,
+            w_qkv.reshape(shard, 3 * head_cols),
+            jnp.concatenate([w_attn_out.T, w_cross_q, w_cross_out.T], axis=1),
+            w_cross_kv.reshape(w_cross_kv.shape[0], 2 * head_cols),
+            w_out.T,
+            w_in.reshape(shard, 2 * unit_cols),
+        ],
+        0,
+    )
+    row_count, model_width = tokens.shape
+    text_rows, text_width = context.shape
+    vec_rows = vec_full.reshape(8, 32, 256)[:, :6, :shard].transpose(1, 0, 2).reshape(6, model_width)
+    gain_rows = vec_rows[:3].astype(jnp.float32)
+    b_in_full = vec_rows[3:5].astype(jnp.float32)
+    b_out_full = vec_rows[5].astype(jnp.float32)
+    ao_t = small_full[:, :head_cols]
+    cross_q_full = small_full[:, head_cols : 2 * head_cols]
+    co_t = small_full[:, 2 * head_cols :]
+    ids = iter(range(2, 12))
+
+    def total(partial_sum):
+        return line_sum(partial_sum.astype(bf), n, next(ids)).astype(jnp.float32)
+
+    def nt(a, b):
+        return lax.dot_general(a, b, (((1,), (1,)), ((), ())), preferred_element_type=jnp.float32)
+
+    def tn(a, b):
+        return lax.dot_general(a, b, (((0,), (0,)), ((), ())), preferred_element_type=jnp.float32)
+
+    head_count = head_cols // HD
+    device_row = lax.axis_index("dp")
+    which_half = device_row % 2
+    clip_index = device_row // 2
+    frame_live = lax.dynamic_index_in_dim(frame_counts, clip_index, 0, keepdims=False)
+    text_live = lax.dynamic_index_in_dim(text_counts, clip_index, 0, keepdims=False)
+    positions = (which_half * row_count + jnp.arange(row_count)).astype(jnp.float32)
+    key_live = jnp.arange(2 * row_count) <= frame_live
+    token_live = jnp.arange(2 * text_rows) < text_live
+    tokens_f = tokens.astype(jnp.float32)
+    grad_y = cotangent.astype(jnp.float32)
+    norm_one, pull_one = jax.vjp(layer_norm, tokens_f, gain_rows[0])
+    h_one = norm_one.astype(bf)
+    qkv = jnp.dot(h_one, qkv_full, preferred_element_type=jnp.float32).reshape(
+        row_count, 3, head_count, HD
+    )
+    queries = rotate(qkv[:, 0], positions).astype(bf)
+    own_keys = rotate(qkv[:, 1], positions).astype(bf).reshape(row_count, head_cols)
+    own_values = qkv[:, 2].astype(bf).reshape(row_count, head_cols)
+    own_text = jnp.dot(context, ckv_full, preferred_element_type=jnp.float32).astype(bf)
+    other = from_partner((own_keys, own_values, own_text), "dp", 0)
+    key_all = in_order(own_keys, other[0], which_half).reshape(2 * row_count, head_count, HD)
+    value_all = in_order(own_values, other[1], which_half).reshape(2 * row_count, head_count, HD)
+    text_all = in_order(own_text, other[2], which_half).reshape(2 * text_rows, 2, head_count, HD)
+    text_keys = text_all[:, 0]
+    text_values = text_all[:, 1]
+    self_attn, self_lse = attend_forward(queries, key_all, value_all, key_live)
+    self_out = self_attn.reshape(row_count, head_cols).astype(bf)
+    x_one = tokens_f + total(nt(self_out, ao_t))
+    norm_two, pull_two = jax.vjp(layer_norm, x_one, gain_rows[1])
+    h_two = norm_two.astype(bf)
+    cross_queries = (
+        jnp.dot(h_two, cross_q_full, preferred_element_type=jnp.float32)
+        .astype(bf)
+        .reshape(row_count, head_count, HD)
+    )
+    cross_attn, cross_lse = attend_forward(cross_queries, text_keys, text_values, token_live)
+    cross_out = cross_attn.reshape(row_count, head_cols).astype(bf)
+    x_two = x_one + total(nt(cross_out, co_t))
+    norm_three, pull_three = jax.vjp(layer_norm, x_two, gain_rows[2])
+    h_three = norm_three.astype(bf)
+    both = (
+        jnp.dot(h_three, in_full, preferred_element_type=jnp.float32).reshape(
+            row_count, 2, unit_cols
+        )
+        + b_in_full
+    )
+    hidden_f, pull_unit = jax.vjp(gated_unit, both)
+    hidden = hidden_f.astype(bf)
+    mixed = (x_two + total(nt(hidden, out_t)) + b_out_full).astype(bf)
+    grad_out_w = tn(cotangent, hidden)
+    grad_b_out = jnp.sum(grad_y, axis=0)
+    grad_hidden = jnp.dot(cotangent, out_t, preferred_element_type=jnp.float32)
+    grad_both = pull_unit(grad_hidden)[0].astype(bf).reshape(row_count, 2 * unit_cols)
+    grad_b_in = jnp.sum(grad_both, axis=0, dtype=jnp.float32).reshape(2, unit_cols)
+    grad_in_w = tn(h_three, grad_both)
+    grad_x_norm, grad_gain_three = pull_three(total(nt(grad_both, in_full)))
+    grad_x_two = grad_y + grad_x_norm
+    grad_two_b = grad_x_two.astype(bf)
+    grad_cross_out_w = tn(grad_two_b, cross_out)
+    grad_cross = (
+        jnp.dot(grad_two_b, co_t, preferred_element_type=jnp.float32)
+        .astype(bf)
+        .reshape(row_count, head_count, HD)
+    )
+    grad_cq, grad_text_key, grad_text_value = attend_backward(
+        cross_queries, text_keys, text_values, token_live, cross_lse, grad_cross
+    )
+    grad_cq_b = grad_cq.reshape(row_count, head_cols).astype(bf)
+    grad_cross_q_w = tn(h_two, grad_cq_b)
+    grad_text = jnp.stack([grad_text_key, grad_text_value], axis=1).reshape(
+        2 * text_rows, 2 * head_cols
+    )
+    grad_x_norm, grad_gain_two = pull_two(total(nt(grad_cq_b, cross_q_full)))
+    grad_x_one = grad_x_two + grad_x_norm
+    grad_one_b = grad_x_one.astype(bf)
+    grad_attn_out_w = tn(grad_one_b, self_out)
+    grad_self = (
+        jnp.dot(grad_one_b, ao_t, preferred_element_type=jnp.float32)
+        .astype(bf)
+        .reshape(row_count, head_count, HD)
+    )
+    grad_query, grad_key_all, grad_value_all = attend_backward(
+        queries, key_all, value_all, key_live, self_lse, grad_self
+    )
+    grad_key_flat = grad_key_all.reshape(2 * row_count, head_cols)
+    grad_value_flat = grad_value_all.reshape(2 * row_count, head_cols)
+    back = from_partner(
+        (
+            partner_rows(grad_key_flat, which_half, row_count),
+            partner_rows(grad_value_flat, which_half, row_count),
+            partner_rows(grad_text, which_half, text_rows),
+        ),
+        "dp",
+        0,
+    )
+    grad_key_own = (own_rows(grad_key_flat, which_half, row_count) + back[0]).reshape(
+        row_count, head_count, HD
+    )
+    grad_value_own = own_rows(grad_value_flat, which_half, row_count) + back[1]
+    grad_text_own = (own_rows(grad_text, which_half, text_rows) + back[2]).astype(bf)
+    grad_query_raw = rotate(grad_query, -positions).reshape(row_count, head_cols)
+    grad_key_raw = rotate(grad_key_own, -positions).reshape(row_count, head_cols)
+    grad_qkv_b = (
+        jnp.stack([grad_query_raw, grad_key_raw, grad_value_own], axis=1)
+        .astype(bf)
+        .reshape(row_count, 3 * head_cols)
+    )
+    grad_qkv_w = tn(h_one, grad_qkv_b)
+    grad_cross_kv_w = tn(context, grad_text_own)
+    grad_x_norm, grad_gain_one = pull_one(total(nt(grad_qkv_b, qkv_full)))
+    grad_tokens = grad_x_one + grad_x_norm
+    grad_small_w = jnp.concatenate([grad_attn_out_w, grad_cross_q_w, grad_cross_out_w], axis=1)
+    g_out, g_in, g_small, g_ckv, g_qkv = scatter_all(
+        [
+            grad_out_w.astype(bf),
+            grad_in_w.astype(bf),
+            grad_small_w.astype(bf),
+            grad_cross_kv_w.astype(bf),
+            grad_qkv_w.astype(bf),
+        ],
+        1,
+    )
+    rows = jnp.concatenate(
+        [grad_gain_one[None], grad_gain_two[None], grad_gain_three[None], grad_b_in, grad_b_out[None]]
+    )
+    vec_sum = lax.psum_scatter(rows, "dp", scatter_dimension=1, tiled=True)
+    return (
+        mixed,
+        grad_tokens,
+        g_qkv.reshape(shard, 3, head_cols),
+        g_small[:, :head_cols].T,
+        g_small[:, head_cols : 2 * head_cols],
+        g_ckv.reshape(-1, 2, head_cols),
+        g_small[:, 2 * head_cols :].T,
+        g_in.reshape(shard, 2, unit_cols),
+        g_out.T,
+        vec_sum[:3],
+        vec_sum[3:5],
+        vec_sum[5],
+    )
 
 
 def body(
@@ -396,4 +948,11 @@
         P(None, ("mp", "dp")),
         P("dp"),
     )
-    return jax.shard_map(body, mesh=mesh, in_specs=in_specs, out_specs=out_specs, check_vma=False)
+    near = mesh.shape["dp"] == 8
+    return jax.shard_map(
+        near_body if near else body,
+        mesh=mesh,
+        in_specs=in_specs,
+        out_specs=out_specs,
+        check_vma=False,
+    )

time: 1630 us -> 758 us (0.47)
  waiting for transfers between devices: 1290 us -> 0.03 us
  Pallas kernels: 0 us -> 519 us
  blocking collectives: 45.1 us -> 0 us
  matrix products: 132 us -> 97.5 us
    psum x5 -> x0, waiting for transfers between devices: 665 us -> none  [the longest x3 433 us: branch_total(): return lax.psum(partial_sum, 'mp')]
    pallas_call x0 -> x8, Pallas kernels: none -> 519 us  [the longest x6 310 us: line_sum(): pl.pallas_call(functools.partial(line_kernel, n), out_shape=jax.ShapeDtyp...]
    reduce_scatter x6 -> x0, waiting for transfers between devices: 413 us -> none  [the longest x1 128 us: body(): lax.psum_scatter(grad_in_w, 'dp', scatter_dimension=0, tiled=True)]
    all_gather x7 -> x0, waiting for transfers between devices: 154 us -> none  [the longest x1 55.3 us: body(): lax.all_gather(w_in, 'dp', axis=0, tiled=True)]
    unnamed x24 -> x2, waiting for transfers between devices: 52.4 us -> 0.02 us
    dot_general x20, matrix products: 104 us -> 67.8 us  [the longest x7 24 us: tn(): lax.dot_general(a, b, (((0,), (0,)), ((), ())), preferred_element_type=jn...]
    dot_general x0 -> x5, local copies, waits for them, and re-layouts: none -> 26.7 us  [the longest x1 12.7 us: near_body(): jnp.dot(h_three, in_full, preferred_element_type=jnp.float32)]
    unnamed x2 -> x0, blocking collectives: 25.7 us -> none
  transfers between devices with their start and end apart: 27 -> 7, of which waited for: 21 -> 0; matrix products, arithmetic and copies ran while one was open for 11% -> 9% of each run, Pallas kernels for 0% -> 14%
where the time goes in v1:
time: 758 us; the launch traced here: 749 us
  Pallas kernels  519 us (68%)
  matrix products  97.5 us (13%)
  local copies, waits for them, and re-layouts  72.1 us (10%)
  other arithmetic  42.7 us (6%)
  between operations  15.7 us (2%)
    pallas_call x6, Pallas kernels, line_sum(): pl.pallas_call(functools.partial(line_kernel, n), out_shape=jax.ShapeDtyp...  310 us
    pallas_call x1, Pallas kernels, scatter_all(): pl.pallas_call(functools.partial(scatter_kernel, count), out_shape=[jax.S...  105 us
    pallas_call x1, Pallas kernels, gather_all(): pl.pallas_call(functools.partial(gather_kernel, count), out_shape=[jax.Sh...  104 us
    dot_general x7, matrix products, tn(): lax.dot_general(a, b, (((0,), (0,)), ((), ())), preferred_element_type=jn...  24 us
    dot_general x6, matrix products, nt(): lax.dot_general(a, b, (((1,), (1,)), ((), ())), preferred_element_type=jn...  21.9 us
    unnamed x181, local copies, waits for them, and re-layouts  19.4 us
  transfers between devices with their start and end apart: 7, of which 0 were waited for; matrix products, arithmetic and copies ran while one was open for 9% of the time, Pallas kernels for 14%

profile of v1, /device:TPU:0, one launch (start us, length us, event | category | flops | bytes accessed | tf_op | source)
XLA Modules:
  0.0 748.7 jit_solution(8636743230173750964)
XLA Ops:
  8.1 1.6 copy.130
  9.7 1.8 copy.129
  11.5 2.4 copy.131
  15.4 104.4 %gather_all.1 = (bf16[8,32,256]{2,1,0:T(8,128)(2,1)}, bf16[8,192,1152]{2,1,0:T(8,128)(2,1)}, bf16[8,192,1152]{2,1,0:T(8,128)(2,1)}, bf16[8,96,768]{2,1,0:T(8,128...) custom-call(bf16[32,256]{1,0:T(8,128)(2,1)} %fusion.68.refs_0_, bf16[192,1152]{1,0:T(8,128)(2,1)} %bitcast.230, ...), custom_call_target="tpu_custom_call" | custom-call | tf_op jit(solution)/shard_map/gather_all/pallas_call | solution.py:103
  119.8 1.6 fusion.47
  123.7 5.8 copy.89
  129.6 4.2 fusion.37
  142.0 12.7 %copy.95 = bf16[3072,1536]{1,0:T(8,128)(2,1)} copy(bf16[3072,1536]{0,1:T(8,128)(2,1)} %bitcast.206) | data formatting | bytes 18874368 | tf_op jit(solution)/shard_map/dot_general | solution.py:597
  156.5 3.6 fusion.6
  160.1 3.0 fusion
  163.2 1.4 log_add_fusion
  164.6 5.0 fusion.44
  170.4 1.0 convolution_convert_fusion.7.x_ref
  171.5 57.8 %line_sum.6 = bf16[512,1536]{1,0:T(8,128)(2,1)S(1)} custom-call(bf16[512,1536]{1,0:T(8,128)(2,1)S(1)} %convolution_convert_fusion.7.x_ref), custom_call_target="tpu_custom_call" | custom-call | tf_op jit(solution)/shard_map/line_sum/pallas_call | solution.py:224
  233.6 1.0 convolution_convert_fusion.6.x_ref
  234.7 53.0 %line_sum.7 = bf16[512,1536]{1,0:T(8,128)(2,1)S(1)} custom-call(bf16[512,1536]{1,0:T(8,128)(2,1)S(1)} %convolution_convert_fusion.6.x_ref), custom_call_target="tpu_custom_call" | custom-call | tf_op jit(solution)/shard_map/line_sum/pallas_call | solution.py:224
  289.0 2.1 slice-done.5
  291.1 7.2 convolution_add_fusion
  298.3 7.0 convolution_convert_fusion.5.x_ref
  305.3 5.3 multiply_bitcast_fusion
  310.6 4.6 convolution_convert_fusion.1
  315.2 48.2 %line_sum.8 = bf16[512,1536]{1,0:T(8,128)(2,1)S(1)} custom-call(bf16[512,1536]{1,0:T(8,128)(2,1)S(1)} %convolution_convert_fusion.5.x_ref), custom_call_target="tpu_custom_call" | custom-call | tf_op jit(solution)/shard_map/line_sum/pallas_call | solution.py:224
  363.5 2.7 convert_reduce_fusion
  366.2 4.7 copy.98
  370.9 9.6 %convolution_convert_fusion.8.x_ref = bf16[512,1536]{1,0:T(8,128)(2,1)S(1)} fusion(bf16[512,3072]{0,1:T(8,128)(2,1)} %bitcast.225, bf16[1536,3072]{1,0:T(8,128)(2,1)} %bitcast.207), kind=kOutput, calls=%fused_computation.80 | convolution fusion | flops 4832624640 | bytes 14155776 | tf_op jit(solution)/shard_map/dot_general | solution.py:550
  380.5 49.5 %line_sum.9 = bf16[512,1536]{1,0:T(8,128)(2,1)S(1)} custom-call(bf16[512,1536]{1,0:T(8,128)(2,1)S(1)} %convolution_convert_fusion.8.x_ref), custom_call_target="tpu_custom_call" | custom-call | tf_op jit(solution)/shard_map/line_sum/pallas_call | solution.py:224
  430.1 1.6 fusion.20
  431.7 2.4 fusion.89
  434.6 1.6 copy-done.34
  437.0 1.1 copy-done.7
  438.1 1.1 convolution_bitcast_fusion.1
  440.2 1.1 fusion.46
  441.7 8.0 %convolution_convert_fusion = bf16[1536,3072]{1,0:T(8,128)(2,1)} fusion(bf16[512,3072]{0,1:T(8,128)(2,1)S(1)} %bitcast.226, f32[512,1536]{1,0:T(8,128)S(1)} %copy-done.5, f32[1536]{0:T(1024)S(1)} %copy-done.49, f32[512]{0:T(512)S(1)} %copy-done.60, f32[512]{0:T(512)S(1)} %copy-done.54), kind=kOutput, calls=%fused_computation.6 | convolution fusion | flops 4839702528 | bytes 15738880 | tf_op jit(solution)/shard_map/dot_general | solution.py:553
  449.7 1.0 convolution_convert_fusion.4.x_ref
  450.8 46.7 %line_sum.10 = bf16[512,1536]{1,0:T(8,128)(2,1)S(1)} custom-call(bf16[512,1536]{1,0:T(8,128)(2,1)S(1)} %convolution_convert_fusion.4.x_ref), custom_call_target="tpu_custom_call" | custom-call | tf_op jit(solution)/shard_map/line_sum/pallas_call | solution.py:224
  498.5 1.9 fusion.21
  500.5 2.9 convert_bitcast_fusion
  503.4 1.7 copy-done.8
  505.0 2.1 convolution_convert_fusion.14
  507.2 3.9 fusion.2
  511.0 8.1 %multiply_reduce_fusion = (f32[6,512]{1,0:T(8,128)S(1)}, f32[6,512,1024]{2,1,0:T(8,128)}) fusion(f32[6,512]{1,0:T(8,128)S(1)} %copy-done.41, f32[6,512,1024]{2,1,0:T(8,128)S(1)} %bitcast.205, pred[1024]{0:T(1024)(128)(4,1)S(1)} %copy-done.71, bf16[512,6,64]{0,2,1:T(8,128)(2,1)S(1)} %bitcast.243, bf16[512,6,64]{0,2,1:T(8,128)(2,1)} %bitcast.11, ...), kind=kOutput, calls=%fused_computation.1 | convolution fusion | flops 421917696 | bytes 26371072 | tf_op jit(solution)/shard_map/while/body/eval_jaxpr/qhd,khd->hqk/dot_general | solution.py:460
  519.1 6.6 multiply_convert_fusion
  525.7 4.3 fusion.42
  530.1 1.2 convolution_multiply_fusion
  531.3 2.6 copy.102
  536.6 2.6 copy.100
  539.2 3.0 copy.104
  542.8 2.5 convolution_convert_fusion.11
  545.3 1.0 convolution_convert_fusion.12
  546.7 1.0 convolution_convert_fusion.10
  547.8 2.1 pad_maximum_fusion.refs_2_
  550.7 2.6 convolution_convert_fusion.9
  554.4 4.2 convolution_convert_fusion.2
  558.6 2.2 convolution_convert_fusion.3.x_ref
  560.9 54.5 %line_sum.11 = bf16[512,1536]{1,0:T(8,128)(2,1)S(1)} custom-call(bf16[512,1536]{1,0:T(8,128)(2,1)S(1)} %convolution_convert_fusion.3.x_ref), custom_call_target="tpu_custom_call" | custom-call | tf_op jit(solution)/shard_map/line_sum/pallas_call | solution.py:224
  616.1 1.5 fusion.22
  617.7 2.8 add_add_fusion.3
  620.5 1.2 copy.121
  621.7 104.8 %scatter_all.1 = (f32[192,1536]{1,0:T(8,128)}, f32[192,3072]{1,0:T(8,128)}, f32[192,1152]{1,0:T(8,128)}, f32[96,768]{1,0:T(8,128)}, f32[192,1152]{1,0:T(8,128)}) custom-call(bf16[4,2,192,1536]{3,2,1,0:T(8,128)(2,1)} %bitcast.218, bf16[4,2,192,3072]{3,2,1,0:T(8,128)(2,1)} %bitcast.211, bf16[4,2,192,1152]{3,2,1,0:T(8,128)(2,1)} %pad_maximum_fusion.refs_2_, ...), custom_call_target="tpu_custom_call" | custom-call | tf_op jit(solution)/shard_map/scatter_all/pallas_call | solution.py:342
  726.5 2.1 slice_bitcast_fusion.2
  728.6 2.1 copy.133
  731.6 4.2 reshape.424
  737.8 1.6 copy.125
  740.7 1.0 copy.135
  (272 shorter events, 35.0 us)
Async XLA Ops:
  7.2 112.6 %copy-start = (bf16[64,768]{1,0:T(8,128)(2,1)S(1)}, bf16[64,768]{1,0:T(8,128)(2,1)}, u32[]{:S(2)}) copy-start(bf16[64,768]{1,0:T(8,128)(2,1)} %param.16) | copy-start | bytes 294916
  7.2 6.7 copy-start.73
  7.2 6.7 copy-start.72
  7.2 7.4 copy-start.38
  7.2 7.3 copy-start.39
  7.2 7.3 copy-start.40
  7.2 728.6 %reduce-scatter.4.cloned.1.call-start = ((), (), s32[]{:S(2)}) async-start(), calls=%async_computation.1 | async-start | bytes 884736
  13.9 108.0 %copy-start.1 = (bf16[512,1536]{1,0:T(8,128)(2,1)S(1)}, bf16[512,1536]{1,0:T(8,128)(2,1)}, u32[]{:S(2)}) copy-start(bf16[512,1536]{1,0:T(8,128)(2,1)} %param.15) | copy-start | bytes 4718596
  121.4 34.7 %collective-permute-start.2 = (bf16[64,768]{1,0:T(8,128)(2,1)S(1)}, bf16[64,768]{1,0:T(8,128)(2,1)S(1)}, u32[]{:S(2)}, u32[]{:S(2)}) collective-permute-start(bf16[64,768]{1,0:T(8,128)(2,1)S(1)} %fusion.47), channel_id=1, source_target_pairs={{0,4},{4,0},{8,12},{12,8},{16,20},{20,16},{24,28},{28,24},{1,5},{5... | collective-permute-start | bytes 294920 | tf_op jit(solution)/shard_map/ppermute | solution.py:374
  122.2 7.3 copy-start.50
  122.8 6.8 copy-start.61
  123.7 5.8 copy-start.42
  133.9 4.9 copy-start.74
  133.9 5.5 copy-start.75
  135.7 20.8 %collective-permute-start.1 = (bf16[512,384]{0,1:T(8,128)(2,1)}, bf16[512,384]{0,1:T(8,128)(2,1)}, u32[]{:S(2)}, u32[]{:S(2)}) collective-permute-start(bf16[512,384]{0,1:T(8,128)(2,1)} %bitcast.15), channel_id=1, source_target_pairs={{0,4},{4,0},{8,12},{12,8},{16,20},{20,16},{24,28},{28,24},{1,5},{5... | collective-permute-start | bytes 1179656 | tf_op jit(solution)/shard_map/ppermute | solution.py:374
  136.5 28.0 %collective-permute-start = (bf16[512,384]{0,1:T(8,128)(2,1)}, bf16[512,384]{0,1:T(8,128)(2,1)}, u32[]{:S(2)}, u32[]{:S(2)}) collective-permute-start(bf16[512,384]{0,1:T(8,128)(2,1)} %bitcast.10), channel_id=1, source_target_pairs={{0,4},{4,0},{8,12},{12,8},{16,20},{20,16},{24,28},{28,24},{1,5},{5... | collective-permute-start | bytes 1179656 | tf_op jit(solution)/shard_map/ppermute | solution.py:374
  137.1 27.5 %copy-start.23 = (bf16[512,6,64]{0,2,1:T(8,128)(2,1)}, bf16[512,6,64]{0,2,1:T(8,128)(2,1)S(1)}, u32[]{:S(2)}) copy-start(bf16[512,6,64]{0,2,1:T(8,128)(2,1)S(1)} %slice_bitcast_fusion.11) | copy-start | bytes 1179652
  142.0 88.4 %copy-start.36 = (f32[1536]{0:T(1024)}, f32[1536]{0:T(1024)S(1)}, u32[]{:S(2)}) copy-start(f32[1536]{0:T(1024)S(1)} %mul.446) | copy-start | bytes 18436
  142.0 14.5 %copy-start.27 = (bf16[512,6,32]{0,2,1:T(8,128)(2,1)S(1)}, bf16[512,6,32]{0,2,1:T(8,128)(2,1)}, u32[]{:S(2)}) copy-start(bf16[512,6,32]{0,2,1:T(8,128)(2,1)} %slice.246) | copy-start | bytes 589828
  142.0 14.5 %copy-start.30 = (bf16[512,6,16]{0,2,1:T(8,128)(2,1)S(1)}, bf16[512,6,16]{0,2,1:T(8,128)(2,1)}, u32[]{:S(2)}) copy-start(bf16[512,6,16]{0,2,1:T(8,128)(2,1)} %get-tuple-element.217) | copy-start | bytes 294916
  155.4 9.1 %copy-start.70 = (pred[1024]{0:T(1024)(128)(4,1)}, pred[1024]{0:T(1024)(128)(4,1)S(1)}, u32[]{:S(2)}) copy-start(pred[1024]{0:T(1024)(128)(4,1)S(1)} %iota_compare_fusion.2) | copy-start | bytes 3076
  160.1 4.5 copy-start.3
  164.6 5.8 copy-start.33
  232.8 56.2 %slice-start.3 = ((s8[9437184]{0:T(1024)(128)(4,1)}), s8[1048576]{0:T(1024)(128)(4,1)S(1)}, s32[]{:S(2)}) async-start(s8[9437184]{0:T(1024)(128)(4,1)} %bitcast.208), calls=%async_computation.5 | async-start | bytes 2097152
  233.6 55.4 %slice-start.4 = ((s8[9437184]{0:T(1024)(128)(4,1)}), s8[4194304]{0:T(1024)(128)(4,1)S(1)}, s32[]{:S(2)}) async-start(s8[9437184]{0:T(1024)(128)(4,1)} %bitcast.208), calls=%async_computation.6 | async-start | bytes 8388608
  287.7 3.3 slice-start.5
  288.5 9.8 %copy-start.4 = (f32[512,1536]{1,0:T(8,128)}, f32[512,1536]{1,0:T(8,128)S(1)}, u32[]{:S(2)}) copy-start(f32[512,1536]{1,0:T(8,128)S(1)} %get-tuple-element.200) | copy-start | bytes 9437188
  288.5 9.7 %copy-start.53 = (f32[512]{0:T(512)}, f32[512]{0:T(512)S(1)}, u32[]{:S(2)}) copy-start(f32[512]{0:T(512)S(1)} %broadcast_multiply_fusion) | copy-start | bytes 6148
  289.0 9.3 %copy-start.67 = (f32[512]{0:T(512)}, f32[512]{0:T(512)S(1)}, u32[]{:S(2)}) copy-start(f32[512]{0:T(512)S(1)} %multiply_reduce_fusion.1) | copy-start | bytes 6148
  289.0 9.3 %copy-start.59 = (f32[512]{0:T(512)}, f32[512]{0:T(512)S(1)}, u32[]{:S(2)}) copy-start(f32[512]{0:T(512)S(1)} %fusion.72) | copy-start | bytes 6148
  298.3 7.0 copy-start.12
  298.3 7.0 copy-start.80
  370.9 59.1 %copy-start.49 = (f32[1536]{0:T(1024)S(1)}, f32[1536]{0:T(1024)}, u32[]{:S(2)}) copy-start(f32[1536]{0:T(1024)} %mul.453) | copy-start | bytes 18436
  370.9 59.1 %copy-start.54 = (f32[512]{0:T(512)S(1)}, f32[512]{0:T(512)}, u32[]{:S(2)}) copy-start(f32[512]{0:T(512)} %copy-done.53) | copy-start | bytes 6148
  370.9 59.1 %copy-start.60 = (f32[512]{0:T(512)S(1)}, f32[512]{0:T(512)}, u32[]{:S(2)}) copy-start(f32[512]{0:T(512)} %copy-done.59) | copy-start | bytes 6148
  380.5 49.6 %copy-start.5 = (f32[512,1536]{1,0:T(8,128)S(1)}, f32[512,1536]{1,0:T(8,128)}, u32[]{:S(2)}) copy-start(f32[512,1536]{1,0:T(8,128)} %copy-done.4) | copy-start | bytes 9437188
  436.2 3.5 copy-start.11
  441.7 8.0 %copy-start.32 = (bf16[6,64,512]{2,1,0:T(8,128)(2,1)}, bf16[6,64,512]{2,1,0:T(8,128)(2,1)S(1)}, u32[]{:S(2)}) copy-start(bf16[6,64,512]{2,1,0:T(8,128)(2,1)S(1)} %fusion.43) | copy-start | bytes 1179652
  449.7 47.8 %copy-start.2 = (bf16[512,1536]{1,0:T(8,128)(2,1)S(1)}, bf16[512,1536]{1,0:T(8,128)(2,1)}, u32[]{:S(2)}) copy-start(bf16[512,1536]{1,0:T(8,128)(2,1)} %param.15) | copy-start | bytes 4718596
  449.7 47.8 %copy-start.37 = (f32[1536]{0:T(1024)S(1)}, f32[1536]{0:T(1024)}, u32[]{:S(2)}) copy-start(f32[1536]{0:T(1024)} %copy-done.36) | copy-start | bytes 18436
  449.7 47.8 %copy-start.47 = (f32[512]{0:T(512)S(1)}, f32[512]{0:T(512)}, u32[]{:S(2)}) copy-start(f32[512]{0:T(512)} %copy-done.46) | copy-start | bytes 6148
  498.5 8.6 %slice-start = ((s8[12582912]{0:T(1024)(128)(4,1)}), s8[4194304]{0:T(1024)(128)(4,1)S(1)}, s32[]{:S(2)}) async-start(s8[12582912]{0:T(1024)(128)(4,1)} %bitcast.204), calls=%async_computation.2 | async-start | bytes 8388608
  500.5 6.7 slice-start.1
  500.5 6.7 slice-start.2
  503.4 3.8 copy-start.41
  503.4 3.8 copy-start.71
  507.2 3.9 copy-start.24
  525.7 4.3 copy-start.28
  525.7 4.3 copy-start.31
  531.3 2.7 copy-start.26
  536.6 14.0 %collective-permute-start.5 = (f32[64,768]{0,1:T(8,128)}, f32[64,768]{0,1:T(8,128)}, u32[]{:S(2)}, u32[]{:S(2)}) collective-permute-start(f32[64,768]{0,1:T(8,128)} %constant_dynamic-slice_fusion), channel_id=1, source_target_pairs={{0,4},{4,0},{8,12},{12,8},{16,20},{20,16},{24,28},{28,24},{1,5},{5... | collective-permute-start | bytes 589832 | tf_op jit(solution)/shard_map/ppermute | solution.py:374
  542.1 3.2 copy-start.20
  542.1 3.2 copy-start.77
  542.2 11.1 %collective-permute-start.3 = (f32[512,384]{0,1:T(8,128)S(1)}, f32[512,384]{0,1:T(8,128)S(1)}, u32[]{:S(2)}, u32[]{:S(2)}) collective-permute-start(f32[512,384]{0,1:T(8,128)S(1)} %constant_dynamic-slice_fusion.2), channel_id=1, source_target_pairs={{0,4},{4,0},{8,12},{12,8},{16,20},{20,16},{24,28},{28,24},{1,5},{5... | collective-permute-start | bytes 2359304 | tf_op jit(solution)/shard_map/ppermute | solution.py:374
  547.8 2.8 copy-start.29
  547.8 3.0 copy-start.16
  549.9 3.6 copy-start.44
  549.9 3.6 copy-start.45
  550.0 3.8 collective-permute-start.4
  554.4 4.2 copy-start.14
  560.9 55.2 %copy-start.64 = (f32[512]{0:T(512)S(1)}, f32[512]{0:T(512)}, u32[]{:S(2)}) copy-start(f32[512]{0:T(512)} %copy-done.63) | copy-start | bytes 6148
  617.7 2.8 copy-start.52
  726.5 4.3 copy-start.35
  730.8 9.9 %copy-start.25 = (f32[192,1536]{1,0:T(8,128)S(1)}, f32[192,1536]{1,0:T(8,128)}, u32[]{:S(2)}) copy-start(f32[192,1536]{1,0:T(8,128)} %get-tuple-element.125) | copy-start | bytes 3538948
  (30 other events, 44.8 us)
Sparse Core Ops, SparseCore 0:
  621.9 45.1 reduce-scatter.3

commit v2 on v0

--- a/solution.py
+++ b/solution.py
@@ -1,12 +1,1335 @@
+import functools
+
 import jax
 import jax.numpy as jnp
 from jax import lax
+from jax.experimental import pallas as pl
+from jax.experimental.pallas import tpu as pltpu
 from jax.sharding import PartitionSpec as P
 
 HD = 64
-
-
+MESH = pl.DeviceIdType.MESH
+HBM = pl.BlockSpec(memory_space=pl.ANY)
+BF = jnp.bfloat16
+F32 = jnp.float32
 epsilon = 1e-05
+CH = 32
+LAG = 2
+DMA = pltpu.SemaphoreType.DMA
+WHOLE = (0, 0)
+
+
+def dot_nn(a, b):
+    return lax.dot_general(a, b, (((1,), (0,)), ((), ())), preferred_element_type=F32)
+
+
+def dot_nt(a, b):
+    return lax.dot_general(a, b, (((1,), (1,)), ((), ())), preferred_element_type=F32)
+
+
+def dot_tn(a, b):
+    return lax.dot_general(a, b, (((0,), (0,)), ((), ())), preferred_element_type=F32)
+
+
+def send(src, dst, send_sem, recv_sem, peer):
+    return pltpu.make_async_remote_copy(
+        src_ref=src,
+        dst_ref=dst,
+        send_sem=send_sem,
+        recv_sem=recv_sem,
+        device_id=peer,
+        device_id_type=MESH,
+    )
+
+
+def rows_at(start, size):
+    return pl.ds(pl.multiple_of(start, 16), size)
+
+
+def greet_all(d, z, n, dp):
+    barrier = pltpu.get_barrier_semaphore()
+    for k in range(1, dp):
+        pl.semaphore_signal(barrier, inc=1, device_id=(jnp.bitwise_xor(d, k), z), device_id_type=MESH)
+
+    @pl.when(z > 0)
+    def _():
+        pl.semaphore_signal(barrier, inc=1, device_id=(d, z - 1), device_id_type=MESH)
+
+    @pl.when(z < n - 1)
+    def _():
+        pl.semaphore_signal(barrier, inc=1, device_id=(d, z + 1), device_id_type=MESH)
+
+    @pl.when((z > 0) & (z < n - 1))
+    def _():
+        pl.semaphore_wait(barrier, dp + 1)
+
+    @pl.when((z == 0) | (z == n - 1))
+    def _():
+        pl.semaphore_wait(barrier, dp)
+
+
+def normal(x):
+    centered = x - jnp.mean(x, axis=-1, keepdims=True)
+    r = lax.rsqrt(jnp.mean(centered * centered, axis=-1, keepdims=True) + epsilon)
+    return centered * r, r
+
+
+class Line:
+    def __init__(self, d, z, n, own, got, dst, base, sems, k, fin):
+        self.d, self.z, self.n = d, z, n
+        self.own, self.got, self.dst, self.base = own, got, dst, base
+        self.sems, self.k, self.fin = sems, k, fin
+        self.half = own.shape[0] // 2
+        self.chunks = self.half // CH
+        self.slots = self.chunks + 2 * LAG * (n - 1)
+        self.next = 0
+
+    def place(self, f):
+        z, n = self.z, self.n
+        return (z, z + 1, z - 1) if f else (n - 1 - z, z - 1, z + 1)
+
+    def fore(self, f, c, nxt):
+        at = rows_at(f * self.half + c * CH, CH)
+        s, r = self.sems[0], self.sems[1]
+        return send(
+            self.own.at[at], self.got.at[at], s.at[self.k, f, c], r.at[self.k, f, c], (self.d, nxt)
+        )
+
+    def back(self, f, c, prv):
+        at = rows_at(self.base + f * self.half + c * CH, CH)
+        s, r = self.sems[2], self.sems[3]
+        return send(
+            self.dst.at[at], self.dst.at[at], s.at[self.k, f, c], r.at[self.k, f, c], (self.d, prv)
+        )
+
+    def slot(self, s):
+        n = self.n
+        for f in range(2):
+            p, nxt, prv = self.place(f)
+            c = s - LAG * p
+            valid = (c >= 0) & (c < self.chunks)
+
+            @pl.when(valid & (p == 0))
+            def _():
+                self.fore(f, c, nxt).start()
+
+            @pl.when(valid & (p > 0))
+            def _():
+                at = rows_at(f * self.half + c * CH, CH)
+                self.fore(f, c, nxt).wait_recv()
+                total = self.own[at].astype(F32) + self.got[at].astype(F32)
+
+                @pl.when(p < n - 1)
+                def _():
+                    self.own[at] = total.astype(BF)
+                    self.fore(f, c, nxt).start()
+
+                @pl.when(p == n - 1)
+                def _():
+                    self.fin(f * self.half + c * CH, total)
+                    self.back(f, c, prv).start()
+
+            b = s - LAG * (2 * (n - 1) - p)
+
+            @pl.when((b >= 0) & (b < self.chunks) & (p < n - 1))
+            def _():
+                self.back(f, b, prv).wait_recv()
+
+                @pl.when(p > 0)
+                def _():
+                    self.back(f, b, prv).start()
+
+    def step(self):
+        self.slot(self.next)
+        self.next += 1
+
+    def left(self):
+        return self.slots - self.next
+
+    def drain(self):
+        def body(c, carry):
+            for f in range(2):
+                p, nxt, prv = self.place(f)
+
+                @pl.when(p < self.n - 1)
+                def _():
+                    self.fore(f, c, nxt).wait_send()
+
+                @pl.when(p > 0)
+                def _():
+                    self.back(f, c, prv).wait_send()
+
+            return carry
+
+        lax.fori_loop(0, self.chunks, body, 0)
+
+
+def run(count, *lines):
+    lines = [line for line in lines if line.next < line.slots]
+    first = [line.next for line in lines]
+
+    def body(s, carry):
+        for line, at in zip(lines, first):
+            line.slot(at + s)
+        return carry
+
+    lax.fori_loop(0, count, body, 0)
+    for line in lines:
+        line.next += count
+
+
+class Gather:
+    def __init__(self, d, z, shard, full, send_sems, recv_sems, local_sems, a):
+        self.d, self.z, self.shard, self.full, self.a = d, z, shard, full, a
+        self.send_sems, self.recv_sems, self.local = send_sems, recv_sems, local_sems
+        self.size = shard.shape[0]
+        self.core, self.xn, self.yn = [(jnp.bitwise_xor(d, k), z) for k in (1, 2, 4)]
+        self.bx, self.by, self.bd = [jnp.bitwise_xor(d, k) for k in (2, 4, 6)]
+        half = self.size // 2
+        self.top, self.bottom = (0, half), (half, half)
+        self.started = []
+
+    def part(self, block, rows):
+        lo, size = rows
+        return self.full.at[rows_at(block * self.size + lo, size or self.size)]
+
+    def copy(self, k, block, rows, peer):
+        part = self.part(block, rows)
+        return send(part, part, self.send_sems.at[self.a, k], self.recv_sems.at[self.a, k], peer)
+
+    def go(self, k, block, rows, peer):
+        cp = self.copy(k, block, rows, peer)
+        cp.start()
+        self.started.append(cp)
+
+    def got(self, k, block, rows, peer):
+        self.copy(k, block, rows, peer).wait_recv()
+
+    def begin(self):
+        for k, peer in ((0, self.xn), (1, self.yn), (2, self.core)):
+            cp = send(
+                self.shard,
+                self.part(self.d, WHOLE),
+                self.send_sems.at[self.a, k],
+                self.recv_sems.at[self.a, k],
+                peer,
+            )
+            cp.start()
+            self.started.append(cp)
+        self.mine = pltpu.make_async_copy(self.shard, self.part(self.d, WHOLE), self.local.at[self.a])
+        self.mine.start()
+
+    def near(self):
+        self.got(0, self.bx, WHOLE, self.xn)
+        self.go(3, self.bx, self.top, self.yn)
+        self.go(5, self.bx, WHOLE, self.core)
+        self.got(1, self.by, WHOLE, self.yn)
+        self.go(4, self.by, self.bottom, self.xn)
+        self.go(6, self.by, WHOLE, self.core)
+
+    def far(self):
+        self.got(3, self.bd, self.top, self.yn)
+        self.go(7, self.bd, self.top, self.core)
+        self.got(4, self.bd, self.bottom, self.xn)
+        self.go(8, self.bd, self.bottom, self.core)
+
+    def last(self):
+        o = [jnp.bitwise_xor(b, 1) for b in (self.d, self.bx, self.by, self.bd)]
+        self.got(2, o[0], WHOLE, self.core)
+        self.got(5, o[1], WHOLE, self.core)
+        self.got(6, o[2], WHOLE, self.core)
+        self.got(7, o[3], self.top, self.core)
+        self.got(8, o[3], self.bottom, self.core)
+        self.mine.wait()
+
+    def drain(self):
+        for cp in self.started:
+            cp.wait_send()
+
+
+class Moves:
+    def __init__(self, sems):
+        self.sems, self.used = sems, 0
+
+    def start(self, src, dst):
+        cp = pltpu.make_async_copy(src, dst, self.sems.at[self.used])
+        self.used += 1
+        cp.start()
+        return cp
+
+
+def turn(u, cosine, low, high):
+    return u * cosine + pltpu.roll(u, 112, 1) * low + pltpu.roll(u, 16, 1) * high
+
+
+def half_mask(rows, e):
+    lane = lax.broadcasted_iota(jnp.int32, (rows, 128), 1)
+    return (lane >= 64) == (e == 1)
+
+
+def softmax(s):
+    w = jnp.exp(s - jnp.max(s, axis=-1, keepdims=True))
+    return w * (1.0 / jnp.sum(w, axis=-1, keepdims=True))
+
+
+FWD_LINES = 4
+
+
+def forward_kernel(
+    n,
+    dp,
+    tokens,
+    context,
+    tables,
+    key_bias,
+    text_bias,
+    vec,
+    s_qkv,
+    s_small,
+    s_ckv,
+    s_out,
+    s_in,
+    w_qkv,
+    w_small,
+    w_out,
+    w_in,
+    o_gv,
+    o_h1,
+    o_q,
+    o_k,
+    o_v,
+    o_p,
+    o_so,
+    o_x1,
+    o_h2,
+    o_cq,
+    o_tkv,
+    o_pc,
+    o_co,
+    o_x2,
+    o_h3,
+    v_vec,
+    gv,
+    v_qkv,
+    v_small,
+    v_ckv,
+    tok,
+    ctx,
+    tab,
+    kb,
+    tb,
+    h1,
+    q,
+    k,
+    v,
+    probs,
+    so,
+    x1,
+    h2,
+    cq,
+    tkv,
+    pc,
+    co,
+    x2,
+    h3,
+    own,
+    got,
+    g_send,
+    g_recv,
+    g_local,
+    v_send,
+    v_recv,
+    k_send,
+    k_recv,
+    fs,
+    fr,
+    bs,
+    br,
+    moves,
+):
+    d = lax.axis_index("dp")
+    z = lax.axis_index("mp")
+    rows = tokens.shape[0]
+    group = rows // 2
+    cols = so.shape[1]
+    pairs = cols // 128
+    half = lax.rem(d, 2)
+    mv = Moves(moves)
+    ld_tok = mv.start(tokens, tok)
+    ld_small = [
+        mv.start(a, b) for a, b in ((context, ctx), (tables, tab), (key_bias, kb), (text_bias, tb))
+    ]
+    ld_vec = mv.start(vec, v_vec.at[d])
+    greet_all(d, z, n, dp)
+    vec_copies = []
+    for j in range(1, dp):
+        peer = (jnp.bitwise_xor(d, j), z)
+        cp = send(vec, v_vec.at[d], v_send.at[j], v_recv.at[j], peer)
+        cp.start()
+        vec_copies.append(cp)
+    gathers = [
+        Gather(d, z, shard, full, g_send, g_recv, g_local, a)
+        for a, (shard, full) in enumerate(
+            ((s_qkv, v_qkv), (s_ckv, v_ckv), (s_small, v_small), (s_out, w_out), (s_in, w_in))
+        )
+    ]
+    g_qkv, g_ckv, g_small, g_out, g_in = gathers
+    g_qkv.begin()
+    ld_tok.wait()
+    ld_vec.wait()
+    for j in range(1, dp):
+        b = jnp.bitwise_xor(d, j)
+        send(v_vec.at[b], v_vec.at[b], v_send.at[j], v_recv.at[j], (b, z)).wait_recv()
+    width = s_qkv.shape[0]
+    for b in range(dp):
+        gv[:, b * width : (b + 1) * width] = v_vec[b][:8, :width].astype(F32)
+
+    def norm_rows(i, carry):
+        at = rows_at(i * CH, CH)
+        nrm, _ = normal(tok[at].astype(F32))
+        h1[at] = (nrm * gv[0:1]).astype(BF)
+        return carry
+
+    lax.fori_loop(0, rows // CH // 2, norm_rows, 0)
+    g_qkv.near()
+    g_ckv.begin()
+    g_small.begin()
+    lax.fori_loop(rows // CH // 2, rows // CH, norm_rows, 0)
+    st = [mv.start(h1, o_h1)]
+    g_qkv.far()
+    g_qkv.last()
+    for ld in ld_small:
+        ld.wait()
+    my_rows = half * rows
+
+    def project(g, carry):
+        at = rows_at(g * group, group)
+        mine = rows_at(my_rows + g * group, group)
+        x = h1[at]
+        for part in (1, 2, 0):
+            u = dot_nn(x, v_qkv[:, part * cols : (part + 1) * cols])
+            if part == 2:
+                v[mine] = u.astype(BF)
+                continue
+            for j in range(pairs):
+                r = turn(u[:, j * 128 : (j + 1) * 128], tab[0, at], tab[1, at], tab[2, at])
+                if part:
+                    k[mine, j * 128 : (j + 1) * 128] = r.astype(BF)
+                else:
+                    q[at, j * 128 : (j + 1) * 128] = (r * HD ** (-0.5)).astype(BF)
+        return carry
+
+    lax.fori_loop(0, 2, project, 0)
+    core = (jnp.bitwise_xor(d, 1), z)
+    mine, theirs = rows_at(my_rows, rows), rows_at((1 - half) * rows, rows)
+    kv = [send(r.at[mine], r.at[mine], k_send.at[i], k_recv.at[i], core) for i, r in enumerate((k, v))]
+    for cp in kv:
+        cp.start()
+    g_ckv.near()
+    g_small.near()
+    g_out.begin()
+    g_ckv.far()
+    g_ckv.last()
+    g_small.far()
+    g_in.begin()
+    text = ctx.shape[0]
+    t_mine, t_theirs = rows_at(half * text, text), rows_at((1 - half) * text, text)
+    tkv[t_mine] = dot_nn(ctx[...], v_ckv[...]).astype(BF)
+    kv.append(send(tkv.at[t_mine], tkv.at[t_mine], k_send.at[2], k_recv.at[2], core))
+    kv[2].start()
+    for i, (r, at) in enumerate(((k, theirs), (v, theirs))):
+        send(r.at[at], r.at[at], k_send.at[i], k_recv.at[i], core).wait_recv()
+    st += [mv.start(v_qkv, w_qkv), mv.start(q, o_q), mv.start(k, o_k), mv.start(v, o_v)]
+
+    def attend(g, queries, keys, key_lo, values, value_lo, bias, save, out, between):
+        at = rows_at(g * group, group)
+
+        def head(h, carry):
+            j, e = h // 2, lax.rem(h, 2)
+            lo = pl.multiple_of(j * 128, 128)
+            mask = half_mask(group, e)
+            qb = jnp.where(mask, queries[at, pl.ds(lo, 128)], jnp.zeros((), BF))
+            s = dot_nt(qb, keys[:, pl.ds(pl.multiple_of(key_lo + lo, 128), 128)]) + bias[0:1]
+            p = softmax(s).astype(BF)
+            save[h, at] = p
+            o = dot_nn(p, values[:, pl.ds(pl.multiple_of(value_lo + lo, 128), 128)])
+            out[at, pl.ds(lo, 128)] = jnp.where(mask, o.astype(BF), out[at, pl.ds(lo, 128)])
+            between(h)
+            return carry
+
+        lax.fori_loop(0, 2 * pairs, head, 0)
+
+    def quiet(h):
+        pass
+
+    def with_line(line, every):
+        first = line.next
+
+        def between(h):
+            if every == 1:
+                line.slot(first + h)
+            else:
+
+                @pl.when(lax.rem(h, every) == 0)
+                def _():
+                    line.slot(first + h // every)
+
+        line.next += -(-2 * pairs // every)
+        return between
+
+    sems = (fs, fr, bs, br)
+
+    def finish_one(g):
+        def fin(lo, total):
+            at = rows_at(g * group + lo, CH)
+            mine = rows_at(g * group // 2 + lax.rem(lo, group // 2), CH)
+            x = tok[at].astype(F32) + total
+            x1[mine] = x
+            h2[at] = (normal(x)[0] * gv[1:2]).astype(BF)
+
+        return fin
+
+    def finish_two(g):
+        def fin(lo, total):
+            at = rows_at(g * group + lo, CH)
+            mine = rows_at(g * group // 2 + lax.rem(lo, group // 2), CH)
+            x = x1[mine] + total
+            x2[mine] = x
+            h3[at] = (normal(x)[0] * gv[2:3]).astype(BF)
+
+        return fin
+
+    one = [
+        Line(d, z, n, own.at[g], got.at[g], h2, g * group, sems, g, finish_one(g)) for g in range(2)
+    ]
+    two = [
+        Line(d, z, n, own.at[2 + g], got.at[2 + g], h3, g * group, sems, 2 + g, finish_two(g))
+        for g in range(2)
+    ]
+
+    def self_part(g):
+        at = rows_at(g * group, group)
+        own[g] = dot_nt(so[at], v_small[:, 0:cols]).astype(BF)
+
+    def cross_project(g):
+        at = rows_at(g * group, group)
+        cq[at] = (dot_nn(h2[at], v_small[:, cols : 2 * cols]) ).astype(BF) * jnp.asarray(HD ** (-0.5), BF)
+
+    def cross_part(g):
+        at = rows_at(g * group, group)
+        own[2 + g] = dot_nt(co[at], v_small[:, 2 * cols :]).astype(BF)
+
+    attend(0, q, k, 0, v, 0, kb, probs, so, quiet)
+    g_small.last()
+    st.append(mv.start(v_small, w_small))
+    self_part(0)
+    st.append(mv.start(probs.at[:, rows_at(0, group)], o_p.at[:, rows_at(0, group)]))
+    attend(1, q, k, 0, v, 0, kb, probs, so, with_line(one[0], 2))
+    self_part(1)
+    st.append(mv.start(probs.at[:, rows_at(group, group)], o_p.at[:, rows_at(group, group)]))
+    st.append(mv.start(so, o_so))
+    run(one[0].left(), one[0], one[1])
+    send(tkv.at[t_theirs], tkv.at[t_theirs], k_send.at[2], k_recv.at[2], core).wait_recv()
+    st.append(mv.start(tkv, o_tkv))
+    cross_project(0)
+    attend(0, cq, tkv, 0, tkv, cols, tb, pc, co, with_line(one[1], 6))
+    cross_part(0)
+    g_out.near()
+    g_in.near()
+    run(one[1].left(), one[1], two[0])
+    cross_project(1)
+    attend(1, cq, tkv, 0, tkv, cols, tb, pc, co, with_line(two[0], 3))
+    cross_part(1)
+    st += [mv.start(h2, o_h2), mv.start(x1, o_x1), mv.start(cq, o_cq), mv.start(pc, o_pc), mv.start(co, o_co)]
+    run(4, two[0], two[1])
+    g_out.far()
+    g_in.far()
+    run(two[0].left(), two[0], two[1])
+    run(two[1].left(), two[1])
+    st += [mv.start(h3, o_h3), mv.start(x2, o_x2), mv.start(gv, o_gv)]
+    g_out.last()
+    g_in.last()
+    for g in gathers:
+        g.drain()
+    for cp in vec_copies + kv:
+        cp.wait_send()
+    for line in one + two:
+        line.drain()
+    for cp in st:
+        cp.wait()
+
+
+def run_forward(n, dp, tokens, context, tables, key_bias, text_bias, vec, s_qkv, s_small, s_ckv, s_out, s_in):
+    rows, width = tokens.shape
+    cols3 = s_qkv.shape[1]
+    cols = cols3 // 3
+    heads = cols // HD
+    text = context.shape[0]
+    half_rows = rows // 2
+    sds = jax.ShapeDtypeStruct
+    outs = [
+        sds((width, cols3), BF),
+        sds((width, cols3), BF),
+        sds((width, s_out.shape[1]), BF),
+        sds((width, s_in.shape[1]), BF),
+        sds((8, width), F32),
+        sds((rows, width), BF),
+        sds((rows, cols), BF),
+        sds((2 * rows, cols), BF),
+        sds((2 * rows, cols), BF),
+        sds((heads, rows, 2 * rows), BF),
+        sds((rows, cols), BF),
+        sds((half_rows, width), F32),
+        sds((rows, width), BF),
+        sds((rows, cols), BF),
+        sds((2 * text, 2 * cols), BF),
+        sds((heads, rows, 2 * text), BF),
+        sds((rows, cols), BF),
+        sds((half_rows, width), F32),
+        sds((rows, width), BF),
+    ]
+    vm = pltpu.VMEM
+    chunks = rows // 4 // CH
+    saved = [vm(o.shape, o.dtype) for o in outs[5:]]
+    scratch = [
+        vm((dp,) + vec.shape, BF),
+        vm((8, width), F32),
+        vm((width, cols3), BF),
+        vm((width, cols3), BF),
+        vm((s_ckv.shape[0] * dp, s_ckv.shape[1]), BF),
+        vm(tokens.shape, BF),
+        vm(context.shape, BF),
+        vm(tables.shape, F32),
+        vm(key_bias.shape, F32),
+        vm(text_bias.shape, F32),
+        *saved,
+        vm((4, half_rows, width), BF),
+        vm((4, half_rows, width), BF),
+        DMA((5, 9)),
+        DMA((5, 9)),
+        DMA((5,)),
+        DMA((dp,)),
+        DMA((dp,)),
+        DMA((3,)),
+        DMA((3,)),
+        *[DMA((FWD_LINES, 2, chunks))] * 4,
+        DMA((32,)),
+    ]
+    return pl.pallas_call(
+        functools.partial(forward_kernel, n, dp),
+        out_shape=outs,
+        in_specs=[HBM] * 11,
+        out_specs=[HBM] * len(outs),
+        scratch_shapes=scratch,
+        compiler_params=pltpu.CompilerParams(
+            collective_id=0, has_side_effects=True, vmem_limit_bytes=58 * 2**20
+        ),
+        name="forward",
+    )(tokens, context, tables, key_bias, text_bias, vec, s_qkv, s_small, s_ckv, s_out, s_in)
+
+
+def backward_kernel(
+    n,
+    dp,
+    tokens,
+    context,
+    cotangent,
+    tables,
+    w_qkv,
+    w_small,
+    w_out,
+    w_in,
+    i_gv,
+    i_h1,
+    i_q,
+    i_k,
+    i_v,
+    i_p,
+    i_so,
+    i_x1,
+    i_h2,
+    i_cq,
+    i_tkv,
+    i_pc,
+    i_co,
+    i_x2,
+    i_h3,
+    o_mixed,
+    o_gt,
+    o_gg,
+    o_out,
+    o_in,
+    o_small,
+    o_ckv,
+    o_qkv,
+    gv,
+    win,
+    wout,
+    wsmall,
+    h2,
+    h3,
+    dy,
+    hid,
+    dgu,
+    dx2r,
+    dx1r,
+    mixed,
+    gt,
+    x1,
+    x2,
+    dx,
+    q,
+    k,
+    v,
+    so,
+    co,
+    cq,
+    dco,
+    dcq,
+    dso,
+    dqkv,
+    tkv,
+    dtkv,
+    pc,
+    pst,
+    dk,
+    dv,
+    ctx,
+    tab,
+    gg,
+    own,
+    got,
+    kst,
+    krv,
+    tst,
+    trv,
+    gst,
+    k_send,
+    k_recv,
+    fs,
+    fr,
+    bs,
+    br,
+    p_sem,
+    g_sem,
+    moves,
+):
+    d = lax.axis_index("dp")
+    z = lax.axis_index("mp")
+    rows, width = tokens.shape
+    group = rows // 2
+    cols = so.shape[1]
+    units = hid.shape[1]
+    pairs = cols // 128
+    half = lax.rem(d, 2)
+    core = (jnp.bitwise_xor(d, 1), z)
+    mv = Moves(moves)
+    first = [mv.start(a, b) for a, b in ((cotangent, dy), (i_gv, gv), (i_h3, h3))]
+    pieces = 2
+    piece = units // pieces
+    w_loads = []
+    for i in range(pieces):
+        at = slice(i * piece, (i + 1) * piece)
+        up = slice(units + i * piece, units + (i + 1) * piece)
+        w_loads.append(
+            [
+                mv.start(w_in.at[:, at], win.at[:, at]),
+                mv.start(w_in.at[:, up], win.at[:, up]),
+                mv.start(w_out.at[:, at], wout.at[:, at]),
+            ]
+        )
+    later = [
+        mv.start(a, b)
+        for a, b in (
+            (i_x2, x2),
+            (w_small, wsmall),
+            (i_x1, x1),
+            (i_h2, h2),
+            (i_co, co),
+            (i_cq, cq),
+            (i_tkv, tkv),
+            (i_pc, pc),
+            (i_q, q),
+            (i_k, k),
+            (i_v, v),
+            (i_so, so),
+            (context, ctx),
+            (tables, tab),
+        )
+    ]
+    greet_all(d, z, n, dp)
+    gg[...] = jnp.zeros_like(gg)
+    dtkv[...] = jnp.zeros_like(dtkv)
+
+    def clear(i, carry):
+        at = rows_at(i * CH, CH)
+        dk[at] = jnp.zeros((CH, cols), F32)
+        dv[at] = jnp.zeros((CH, cols), F32)
+        return carry
+
+    lax.fori_loop(0, 2 * rows // CH, clear, 0)
+    for cp in first:
+        cp.wait()
+
+    def bias_sum(i, carry):
+        gg[5:6] += jnp.sum(dy[rows_at(i * CH, CH)].astype(F32), axis=0, keepdims=True)
+        return carry
+
+    lax.fori_loop(0, rows // CH, bias_sum, 0)
+    tile = 256
+
+    def feed(g, lo, count, between):
+        at = rows_at(g * group, group)
+
+        def step(i, carry):
+            u = pl.multiple_of(i * tile, tile)
+            us, ups = pl.ds(u, tile), pl.ds(pl.multiple_of(units + u, tile), tile)
+            x = h3[at]
+            gate = dot_nn(x, win[:, us]) + gv[3:4, us]
+            up = dot_nn(x, win[:, ups]) + gv[4:5, us]
+            dh = dot_nn(dy[at], wout[:, us])
+            sig = jax.nn.sigmoid(gate)
+            act = gate * sig
+            hid[at, us] = (act * up).astype(BF)
+            d_gate = (dh * up * (sig * (1.0 + gate * (1.0 - sig)))).astype(BF)
+            d_up = (dh * act).astype(BF)
+            dgu[at, us] = d_gate
+            dgu[at, ups] = d_up
+            gg[3:4, us] += jnp.sum(d_gate.astype(F32), axis=0, keepdims=True)
+            gg[4:5, us] += jnp.sum(d_up.astype(F32), axis=0, keepdims=True)
+            between(i)
+            return carry
+
+        lax.fori_loop(lo, lo + count, step, 0)
+
+    def norm_back(x, dn, gain, row):
+        nrm, r = normal(x)
+        gg[row : row + 1] += jnp.sum(dn * nrm, axis=0, keepdims=True)
+        e = dn * gain
+        return r * (
+            e
+            - jnp.mean(e, axis=-1, keepdims=True)
+            - nrm * jnp.mean(e * nrm, axis=-1, keepdims=True)
+        )
+
+    def places(g, lo):
+        return rows_at(g * group + lo, CH), rows_at(
+            g * group // 2 + lax.rem(lo, group // 2), CH
+        )
+
+    def finish_mixed(g):
+        def fin(lo, total):
+            at, mine = places(g, lo)
+            mixed[at] = (x2[mine] + total + gv[5:6]).astype(BF)
+
+        return fin
+
+    def finish_three(g):
+        def fin(lo, total):
+            at, mine = places(g, lo)
+            x = dy[at].astype(F32) + norm_back(x2[mine], total, gv[2:3], 2)
+            dx[mine] = x
+            dx2r[at] = x.astype(BF)
+
+        return fin
+
+    def finish_two(g):
+        def fin(lo, total):
+            at, mine = places(g, lo)
+            x = dx[mine] + norm_back(x1[mine], total, gv[1:2], 1)
+            dx[mine] = x
+            dx1r[at] = x.astype(BF)
+
+        return fin
+
+    def finish_one(g):
+        def fin(lo, total):
+            at, mine = places(g, lo)
+            x = dx[mine] + norm_back(h3[at].astype(F32), total, gv[0:1], 0)
+            gt[at] = x.astype(BF)
+
+        return fin
+
+    sems = (fs, fr, bs, br)
+
+    def lines(dst, slot, index, fin):
+        return [
+            Line(
+                d, z, n, own.at[slot + g], got.at[slot + g], dst, g * group, sems, index + g, fin(g)
+            )
+            for g in range(2)
+        ]
+
+    mix = lines(mixed, 2, 0, finish_mixed)
+    three = lines(dx2r, 0, 2, finish_three)
+    two = lines(dx1r, 0, 4, finish_two)
+    one = lines(gt, 0, 6, finish_one)
+
+    def quiet(i):
+        pass
+
+    def with_lines(total, every, *ls):
+        ls = [line for line in ls if line.next < line.slots]
+        starts = [line.next for line in ls]
+
+        def between(i):
+            def go():
+                for line, s in zip(ls, starts):
+                    line.slot(s + i // every)
+
+            if every == 1:
+                go()
+            else:
+                pl.when(lax.rem(i, every) == 0)(go)
+
+        for line in ls:
+            line.next += -(-total // every)
+        return between
+
+    tiles = units // tile
+    per = tiles // pieces
+
+    def grads(left, right, lo, size, out, out_lo, between):
+        step_rows = 384
+        steps = left.shape[1] // step_rows
+
+        def out_copy(t, slot):
+            return pltpu.make_async_copy(
+                gst.at[slot, :, pl.ds(0, size)],
+                out.at[pl.ds(pl.multiple_of(t * step_rows, 16), step_rows), pl.ds(out_lo, size)],
+                g_sem.at[slot],
+            )
+
+        def step(t, carry):
+            slot = lax.rem(t, 2)
+
+            @pl.when(t >= 2)
+            def _():
+                out_copy(t - 2, slot).wait()
+
+            part = dot_tn(
+                left[:, pl.ds(pl.multiple_of(t * step_rows, 128), step_rows)],
+                right[:, lo : lo + size],
+            )
+            gst[slot, :, 0:size] = part.astype(BF)
+            out_copy(t, slot).start()
+            between(t)
+            return carry
+
+        lax.fori_loop(0, steps, step, 0)
+        for t in range(max(0, steps - 2), steps):
+            out_copy(t, t % 2).wait()
+
+    def attend_back(g, d_out, queries, keys, key_lo, values, value_lo, probs, dkr, dk_lo, dvr, dv_lo, dq, between):
+        at = rows_at(g * group, group)
+
+        def head(h, carry):
+            j, e = h // 2, lax.rem(h, 2)
+            lo = pl.multiple_of(j * 128, 128)
+            here = pl.ds(lo, 128)
+            mask = half_mask(group, e)
+            zero = jnp.zeros((), BF)
+            do = jnp.where(mask, d_out[at, here], zero)
+            qb = jnp.where(mask, queries[at, here], zero)
+            p = probs(h)
+            pf = p.astype(F32)
+            dp_ = dot_nt(do, values[:, pl.ds(pl.multiple_of(value_lo + lo, 128), 128)])
+            ds = (pf * (dp_ - jnp.sum(pf * dp_, axis=-1, keepdims=True))).astype(BF)
+            g_q = dot_nn(ds, keys[:, pl.ds(pl.multiple_of(key_lo + lo, 128), 128)]) * HD ** (-0.5)
+            dkr[:, pl.ds(pl.multiple_of(dk_lo + lo, 128), 128)] += dot_tn(ds, qb)
+            dvr[:, pl.ds(pl.multiple_of(dv_lo + lo, 128), 128)] += dot_tn(p, do)
+            dq(h, at, here, mask, g_q)
+            between(h)
+            return carry
+
+        lax.fori_loop(0, 2 * pairs, head, 0)
+
+    def cross_back(g, between):
+        at = rows_at(g * group, group)
+        dco[at] = dot_nn(dx2r[at], wsmall[:, 2 * cols :]).astype(BF)
+
+        def dq(h, at, here, mask, g_q):
+            dcq[at, here] = jnp.where(mask, g_q.astype(BF), dcq[at, here])
+
+        attend_back(
+            g, dco, cq, tkv, 0, tkv, cols, lambda h: pc[h, at], dtkv, 0, dtkv, cols, dq, between
+        )
+
+    def self_back(g, between):
+        at = rows_at(g * group, group)
+
+        def load(h):
+            slot = lax.rem(h, 2)
+            return pltpu.make_async_copy(i_p.at[h, at], pst.at[slot], p_sem.at[slot])
+
+        load(0).start()
+        dso[at] = dot_nn(dx1r[at], wsmall[:, 0:cols]).astype(BF)
+
+        def probs(h):
+            @pl.when(h + 1 < 2 * pairs)
+            def _():
+                load(h + 1).start()
+
+            load(h).wait()
+            return pst[lax.rem(h, 2)]
+
+        def dq(h, at, here, mask, g_q):
+            r = turn(g_q, tab[0, at], -tab[1, at], -tab[2, at]).astype(BF)
+            dqkv[at, here] = jnp.where(mask, r, dqkv[at, here])
+
+        attend_back(g, dso, q, k, 0, v, 0, probs, dk, 0, dv, 0, dq, between)
+
+    def three_part(g):
+        at = rows_at(g * group, group)
+        own[g] = dot_nt(dgu[at], win[...]).astype(BF)
+
+    def down_part(g):
+        at = rows_at(g * group, group)
+        own[2 + g] = dot_nt(hid[at], wout[...]).astype(BF)
+
+    def two_part(g):
+        at = rows_at(g * group, group)
+        own[g] = dot_nt(dcq[at], wsmall[:, cols : 2 * cols]).astype(BF)
+
+    def one_part(g):
+        at = rows_at(g * group, group)
+        own[g] = dot_nt(dqkv[at], win[:, 0 : 3 * cols]).astype(BF)
+
+    for i in range(pieces):
+        for cp in w_loads[i]:
+            cp.wait()
+        feed(0, i * per, per, quiet)
+    three_part(0)
+    for cp in later:
+        cp.wait()
+    feed(1, 0, tiles, with_lines(tiles, 1, three[0]))
+    three_part(1)
+    down_part(0)
+    run(1, three[0], three[1])
+    down_part(1)
+    ld_qkv = mv.start(w_qkv, win.at[:, pl.ds(0, 3 * cols)])
+    run(1, three[0], three[1])
+    grads(dy, hid, 0, units, o_out, 0, with_lines(4, 1, three[0], three[1]))
+    grads(h3, dgu, 0, units, o_in, 0, with_lines(4, 1, three[0], three[1]))
+    run(three[0].left(), three[0], three[1])
+    ld_h1 = mv.start(i_h1, hid)
+    cross_back(0, with_lines(6, 3, three[1]))
+    three[0].drain()
+    two_part(0)
+    run(three[1].left(), three[1], two[0])
+    cross_back(1, with_lines(6, 3, two[0]))
+    three[1].drain()
+    two_part(1)
+    text = ctx.shape[0]
+    t_mine, t_theirs = rows_at(half * text, text), rows_at((1 - half) * text, text)
+    tst[...] = dtkv[t_theirs].astype(BF)
+    t_copy = send(tst, trv, k_send.at[2], k_recv.at[2], core)
+    t_copy.start()
+    grads(h3, dgu, units, units, o_in, units, with_lines(4, 1, two[0], two[1]))
+    ld_tok = mv.start(tokens, h3)
+    grads(dx2r, co, 0, cols, o_small, 2 * cols, with_lines(4, 2, two[0], two[1]))
+    grads(h2, dcq, 0, cols, o_small, cols, with_lines(4, 2, two[0], two[1]))
+    run(two[0].left(), two[0], two[1])
+    self_back(0, with_lines(6, 1, two[1]))
+    two[0].drain()
+    run(two[1].left(), two[1])
+    self_back(1, with_lines(6, 1, mix[0], mix[1]))
+    two[1].drain()
+    mine, theirs = rows_at(half * rows, rows), rows_at((1 - half) * rows, rows)
+    kst[0] = dk[theirs].astype(BF)
+    k_copy = send(kst.at[0], krv.at[0], k_send.at[0], k_recv.at[0], core)
+    k_copy.start()
+    kst[1] = dv[theirs].astype(BF)
+    v_copy = send(kst.at[1], krv.at[1], k_send.at[1], k_recv.at[1], core)
+    v_copy.start()
+    ld_h1.wait()
+    ld_qkv.wait()
+    ld_tok.wait()
+    k_copy.wait_recv()
+    for g in range(2):
+        at = slice(g * group, (g + 1) * group)
+        own_at = rows_at(half * rows + g * group, group)
+        for j in range(pairs):
+            here = slice(j * 128, (j + 1) * 128)
+            u = dk[own_at, here] + krv[0, at, here].astype(F32)
+            dqkv[at, cols + j * 128 : cols + (j + 1) * 128] = turn(
+                u, tab[0, at], -tab[1, at], -tab[2, at]
+            ).astype(BF)
+        if g == 0:
+            v_copy.wait_recv()
+        dqkv[at, 2 * cols :] = (dv[own_at] + krv[1, at].astype(F32)).astype(BF)
+        one_part(g)
+        if g == 0:
+            run(2, one[0], mix[0], mix[1])
+    grads(dx1r, so, 0, cols, o_small, 0, with_lines(4, 1, one[0], one[1], mix[0], mix[1]))
+    grads(hid, dqkv, 0, 3 * cols, o_qkv, 0, with_lines(4, 1, one[0], one[1], mix[0], mix[1]))
+    t_copy.wait()
+    tst[...] = (dtkv[t_mine] + trv[...].astype(F32)).astype(BF)
+    grads(ctx, tst, 0, 2 * cols, o_ckv, 0, with_lines(2, 1, one[0], one[1], mix[0], mix[1]))
+    run(one[1].left() - 2, one[0], one[1], mix[0], mix[1])
+    st = [mv.start(gg, o_gg), mv.start(mixed, o_mixed)]
+    run(one[1].left(), one[1])
+    st.append(mv.start(gt, o_gt))
+    k_copy.wait_send()
+    v_copy.wait_send()
+    for line in mix + one:
+        line.drain()
+    for cp in st:
+        cp.wait()
+
+
+def run_backward(n, dp, tokens, context, cotangent, tables, saved):
+    rows, width = tokens.shape
+    w_qkv, w_in = saved[0], saved[3]
+    cols = w_qkv.shape[1] // 3
+    units = w_in.shape[1] // 2
+    heads = cols // HD
+    text, text_width = context.shape
+    half_rows = rows // 2
+    sds = jax.ShapeDtypeStruct
+    outs = [
+        sds((rows, width), BF),
+        sds((rows, width), BF),
+        sds((8, width), F32),
+        sds((width, units), BF),
+        sds((width, 2 * units), BF),
+        sds((width, 3 * cols), BF),
+        sds((text_width, 2 * cols), BF),
+        sds((width, 3 * cols), BF),
+    ]
+    vm = pltpu.VMEM
+    chunks = rows // 4 // CH
+    full, head, own_x = vm((rows, width), BF), vm((rows, cols), BF), vm((half_rows, width), F32)
+    keys = vm((2 * rows, cols), BF)
+    scratch = [
+        vm((8, width), F32),
+        vm((width, 2 * units), BF),
+        vm((width, units), BF),
+        vm((width, 3 * cols), BF),
+        full,
+        full,
+        full,
+        vm((rows, units), BF),
+        vm((rows, 2 * units), BF),
+        full,
+        full,
+        full,
+        full,
+        own_x,
+        own_x,
+        own_x,
+        head,
+        keys,
+        keys,
+        head,
+        head,
+        head,
+        head,
+        head,
+        head,
+        vm((rows, 3 * cols), BF),
+        vm((2 * text, 2 * cols), BF),
+        vm((2 * text, 2 * cols), F32),
+        vm((heads, rows, 2 * text), BF),
+        vm((2, half_rows, 2 * rows), BF),
+        vm((2 * rows, cols), F32),
+        vm((2 * rows, cols), F32),
+        vm(context.shape, BF),
+        vm(tables.shape, F32),
+        vm((8, width), F32),
+        vm((4, half_rows, width), BF),
+        vm((4, half_rows, width), BF),
+        vm((2, rows, cols), BF),
+        vm((2, rows, cols), BF),
+        vm((text, 2 * cols), BF),
+        vm((text, 2 * cols), BF),
+        vm((2, 384, units), BF),
+        DMA((3,)),
+        DMA((3,)),
+        *[DMA((8, 2, chunks))] * 4,
+        DMA((2,)),
+        DMA((2,)),
+        DMA((40,)),
+    ]
+    ins = (tokens, context, cotangent, tables, *saved)
+    return pl.pallas_call(
+        functools.partial(backward_kernel, n, dp),
+        out_shape=outs,
+        in_specs=[HBM] * len(ins),
+        out_specs=[HBM] * len(outs),
+        scratch_shapes=scratch,
+        compiler_params=pltpu.CompilerParams(
+            collective_id=1, has_side_effects=True, vmem_limit_bytes=63 * 2**20
+        ),
+        name="backward",
+    )(*ins)
+
+
+def scatter_kernel(count, *refs):
+    ins, outs = refs[:count], refs[count : 2 * count]
+    rest = refs[2 * count :]
+    own, got, one, two, out_v = [rest[i * count : (i + 1) * count] for i in range(5)]
+    send_sems, recv_sems, local_sems = rest[5 * count :]
+    d = lax.axis_index("dp")
+    m = lax.axis_index("mp")
+    core, xn, yn = [(jnp.bitwise_xor(d, k), m) for k in (1, 2, 4)]
+    c = lax.rem(d, 2)
+    x = lax.rem(d // 2, 2)
+    y = d // 4
+    barrier = pltpu.get_barrier_semaphore()
+    for peer in (core, xn, yn):
+        pl.semaphore_signal(barrier, inc=1, device_id=peer, device_id_type=MESH)
+    pl.semaphore_wait(barrier, 3)
+    copies = [{} for _ in range(count)]
+    loads, stores = [], []
+
+    def go(a, k, src, dst, peer):
+        cp = send(src, dst, send_sems.at[a, k], recv_sems.at[a, k], peer)
+        cp.start()
+        copies[a][k] = cp
+
+    for a in range(count):
+        go(a, 0, ins[a].at[:, 1 - c], got[a], core)
+        cp = pltpu.make_async_copy(ins[a].at[:, c], own[a], local_sems.at[a])
+        cp.start()
+        loads.append(cp)
+
+    def add_core(a):
+        loads[a].wait()
+        copies[a][0].wait_recv()
+        rows = own[a].shape[1]
+
+        def tile(i, carry):
+            j, t = i // (rows // 16), lax.rem(i, rows // 16)
+            at = pl.ds(pl.multiple_of(t * 16, 16), 16)
+            own[a][j, at] = (own[a][j, at].astype(jnp.float32) + got[a][j, at].astype(jnp.float32)).astype(
+                jnp.bfloat16
+            )
+            return carry
+
+        lax.fori_loop(0, 4 * (rows // 16), tile, 0)
+        half = rows // 2
+        top, bottom = pl.ds(0, half), pl.ds(half, half)
+        for b in range(2):
+            go(a, 1 + b, own[a].at[2 * b + 1 - x, top], one[a].at[0, b], xn)
+            go(a, 3 + b, own[a].at[2 * (1 - y) + b, bottom], one[a].at[1, b], yn)
+
+    def plus(a, at_block, lo, part):
+        half = own[a].shape[1] // 2
+
+        def tile(t, carry):
+            at = pl.ds(pl.multiple_of(lo + t * 16, 16), 16)
+            frm = pl.ds(pl.multiple_of(t * 16, 16), 16)
+            own[a][at_block, at] = (
+                own[a][at_block, at].astype(jnp.float32) + part[frm].astype(jnp.float32)
+            ).astype(jnp.bfloat16)
+            return carry
+
+        lax.fori_loop(0, half // 16, tile, 0)
+
+    def add_one(a):
+        half = own[a].shape[1] // 2
+        top, bottom = pl.ds(0, half), pl.ds(half, half)
+        for b in range(2):
+            copies[a][1 + b].wait_recv()
+            plus(a, 2 * b + x, 0, one[a].at[0, b])
+            copies[a][3 + b].wait_recv()
+            plus(a, 2 * y + b, half, one[a].at[1, b])
+        go(a, 5, own[a].at[2 * (1 - y) + x, top], two[a].at[0], yn)
+        go(a, 6, own[a].at[2 * y + 1 - x, bottom], two[a].at[1], xn)
+
+    def add_two(a):
+        half = own[a].shape[1] // 2
+        for part in range(2):
+            copies[a][5 + part].wait_recv()
+
+            def tile(t, carry, part=part):
+                at = pl.ds(pl.multiple_of(part * half + t * 16, 16), 16)
+                frm = pl.ds(pl.multiple_of(t * 16, 16), 16)
+                out_v[a][at] = own[a][2 * y + x, at].astype(jnp.float32) + two[a][part, frm].astype(jnp.float32)
+                return carry
+
+            lax.fori_loop(0, half // 16, tile, 0)
+        cp = pltpu.make_async_copy(out_v[a], outs[a], local_sems.at[a])
+        cp.start()
+        stores.append(cp)
+
+    for s in range(count + 2):
+        if s < count:
+            add_core(s)
+        if 0 <= s - 1 < count:
+            add_one(s - 1)
+        if 0 <= s - 2 < count:
+            add_two(s - 2)
+    for a in range(count):
+        for cp in copies[a].values():
+            cp.wait_send()
+    for cp in stores:
+        cp.wait()
+
+
+def scatter_all(arrays, collective_id):
+    count = len(arrays)
+    views = [a.reshape(4, 2, a.shape[0] // 8, a.shape[1]) for a in arrays]
+    sizes = [v.shape[2:] for v in views]
+    bf = jnp.bfloat16
+    return pl.pallas_call(
+        functools.partial(scatter_kernel, count),
+        out_shape=[jax.ShapeDtypeStruct(s, jnp.float32) for s in sizes],
+        in_specs=[HBM] * count,
+        out_specs=[HBM] * count,
+        scratch_shapes=[pltpu.VMEM((4,) + s, bf) for s in sizes]
+        + [pltpu.VMEM((4,) + s, bf) for s in sizes]
+        + [pltpu.VMEM((2, 2, s[0] // 2, s[1]), bf) for s in sizes]
+        + [pltpu.VMEM((2, s[0] // 2, s[1]), bf) for s in sizes]
+        + [pltpu.VMEM(s, jnp.float32) for s in sizes]
+        + [
+            pltpu.SemaphoreType.DMA((count, 7)),
+            pltpu.SemaphoreType.DMA((count, 7)),
+            pltpu.SemaphoreType.DMA((count,)),
+        ],
+        compiler_params=pltpu.CompilerParams(
+            collective_id=collective_id, has_side_effects=True, vmem_limit_bytes=60 * 2**20
+        ),
+        name="scatter_all",
+    )(*views)
+
+
+def prepare(tokens, context, frame_counts, text_counts, w_qkv, w_attn_out, w_cross_q, w_cross_kv, w_cross_out, w_in, w_out, norm_gains, b_in, b_out):
+    shard, _, cols = w_qkv.shape
+    rows = tokens.shape[0]
+    text = context.shape[0]
+    vec = jnp.concatenate([norm_gains, b_in, b_out[None]], axis=0)
+    vec = jnp.pad(vec, ((0, 16 - vec.shape[0]), (0, 256 - shard)))
+    d = lax.axis_index("dp")
+    clip, half = d // 2, d % 2
+    frames = lax.dynamic_index_in_dim(frame_counts, clip, 0, keepdims=False)
+    texts = lax.dynamic_index_in_dim(text_counts, clip, 0, keepdims=False)
+    key_bias = jnp.where(jnp.arange(2 * rows) <= frames, 0.0, -1e30).astype(F32)[None]
+    text_bias = jnp.where(jnp.arange(2 * text) < texts, 0.0, -1e30).astype(F32)[None]
+    m = HD // 4
+    lane = jnp.arange(128) % HD
+    frequency = 10000.0 ** (-(lane % m).astype(F32) / m)
+    angle = (half * rows + jnp.arange(rows)).astype(F32)[:, None] * frequency[None]
+    sine = jnp.sin(angle)
+    tables = jnp.stack(
+        [
+            jnp.where(lane < 2 * m, jnp.cos(angle), 1.0),
+            jnp.where(lane < m, -sine, 0.0),
+            jnp.where((lane >= m) & (lane < 2 * m), sine, 0.0),
+        ]
+    )
+    return (
+        tables,
+        jnp.broadcast_to(key_bias, (8, 2 * rows)),
+        jnp.broadcast_to(text_bias, (8, 2 * text)),
+        vec,
+        w_qkv.reshape(shard, 3 * cols),
+        jnp.concatenate([w_attn_out.T, w_cross_q, w_cross_out.T], axis=1),
+        w_cross_kv.reshape(w_cross_kv.shape[0], 2 * cols),
+        w_out.T,
+        w_in.reshape(shard, -1),
+    )
 
 
 def from_partner(block, axis, stride):
@@ -364,6 +1687,61 @@
     )
 
 
+def near_body(
+    tokens,
+    context,
+    frame_counts,
+    text_counts,
+    w_qkv,
+    w_attn_out,
+    w_cross_q,
+    w_cross_kv,
+    w_cross_out,
+    w_in,
+    w_out,
+    norm_gains,
+    b_in,
+    b_out,
+    cotangent,
+):
+    n, dp = lax.axis_size("mp"), lax.axis_size("dp")
+    shard, _, cols = w_qkv.shape
+    tables, key_bias, text_bias, vec, *shards = prepare(
+        tokens,
+        context,
+        frame_counts,
+        text_counts,
+        w_qkv,
+        w_attn_out,
+        w_cross_q,
+        w_cross_kv,
+        w_cross_out,
+        w_in,
+        w_out,
+        norm_gains,
+        b_in,
+        b_out,
+    )
+    saved = run_forward(n, dp, tokens, context, tables, key_bias, text_bias, vec, *shards)
+    mixed, gt, gg, *parts = run_backward(n, dp, tokens, context, cotangent, tables, saved)
+    g_out, g_in, g_small, g_ckv, g_qkv = scatter_all(parts, 2)
+    vec_sum = lax.psum_scatter(gg, "dp", scatter_dimension=1, tiled=True)
+    return (
+        mixed,
+        gt.astype(F32),
+        g_qkv.reshape(shard, 3, cols),
+        g_small[:, :cols].T,
+        g_small[:, cols : 2 * cols],
+        g_ckv.reshape(-1, 2, cols),
+        g_small[:, 2 * cols :].T,
+        g_in.reshape(shard, 2, -1),
+        g_out.T,
+        lax.psum(vec_sum[:3], "mp"),
+        vec_sum[3:5],
+        vec_sum[5],
+    )
+
+
 def solution(mesh):
     in_specs = (
         P("dp", None),
@@ -396,4 +1774,11 @@
         P(None, ("mp", "dp")),
         P("dp"),
     )
-    return jax.shard_map(body, mesh=mesh, in_specs=in_specs, out_specs=out_specs, check_vma=False)
+    near = mesh.shape["dp"] == 8
+    return jax.shard_map(
+        near_body if near else body,
+        mesh=mesh,
+        in_specs=in_specs,
+        out_specs=out_specs,
+        check_vma=False,
+    )

time: 1630 us -> 520 us (0.32)
  waiting for transfers between devices: 1290 us -> 0.02 us
  Pallas kernels: 0 us -> 455 us
  matrix products: 132 us -> 0 us
  local copies, waits for them, and re-layouts: 77 us -> 26.2 us
  other arithmetic: 55.6 us -> 6.75 us
  blocking collectives: 45.1 us -> 8.94 us
    psum x5 -> x0, waiting for transfers between devices: 665 us -> none  [the longest x3 433 us: branch_total(): return lax.psum(partial_sum, 'mp')]
    pallas_call x0 -> x3, Pallas kernels: none -> 455 us  [the longest x1 206 us: run_backward(): pl.pallas_call(functools.partial(backward_kernel, n, dp), out_shape=outs,...]
    reduce_scatter x6 -> x0, waiting for transfers between devices: 413 us -> none  [the longest x1 128 us: body(): lax.psum_scatter(grad_in_w, 'dp', scatter_dimension=0, tiled=True)]
    all_gather x7 -> x0, waiting for transfers between devices: 154 us -> none  [the longest x1 55.3 us: body(): lax.all_gather(w_in, 'dp', axis=0, tiled=True)]
    dot_general x32 -> x0, matrix products: 132 us -> none  [the longest x1 11.4 us: body(): jnp.dot(h_three, in_full.reshape(model_width, 2 * unit_cols), preferred_e...]
    unnamed x24 -> x2, waiting for transfers between devices: 52.4 us -> 0.02 us
    unnamed x212 -> x30, local copies, waits for them, and re-layouts: 40.4 us -> 10.9 us
    reduce_sum x16 -> x0, other arithmetic: 29.4 us -> none  [the longest x4 13.6 us: layer_norm(): return centered * lax.rsqrt(spread + epsilon) * gain_row]
  transfers between devices with their start and end apart: 27 -> 1, of which waited for: 21 -> 0; matrix products, arithmetic and copies ran while one was open for 11% -> 2% of each run, Pallas kernels for 0% -> 20%
where the time goes in v2:
time: 520 us; the launch traced here: 511 us
  Pallas kernels  455 us (88%)
  local copies, waits for them, and re-layouts  26.2 us (5%)
  between operations  14.6 us (3%)
  blocking collectives  8.94 us (2%)
  other arithmetic  6.75 us (1%)
    pallas_call x1, Pallas kernels, run_backward(): pl.pallas_call(functools.partial(backward_kernel, n, dp), out_shape=outs,...  206 us
    pallas_call x1, Pallas kernels, run_forward(): pl.pallas_call(functools.partial(forward_kernel, n, dp), out_shape=outs,...  146 us
    pallas_call x1, Pallas kernels, scatter_all(): pl.pallas_call(functools.partial(scatter_kernel, count), out_shape=[jax.S...  104 us
    unnamed x30, local copies, waits for them, and re-layouts  10.9 us
  transfers between devices with their start and end apart: 1, of which 0 were waited for; matrix products, arithmetic and copies ran while one was open for 2% of the time, Pallas kernels for 20%

profile of v2, /device:TPU:0, one launch (start us, length us, event | category | flops | bytes accessed | tf_op | source)
XLA Modules:
  0.0 511.3 jit_solution(9299458967583959953)
XLA Ops:
  7.2 0.0 copy-start.2
  7.2 0.0 reduce-scatter.4.cloned.1.call-start
  7.3 1.3 dynamic_slice.8
  8.6 0.6 compare_select_fusion.2
  9.3 1.2 dynamic_slice.7
  10.5 0.7 broadcast_in_dim.62
  11.2 0.6 fusion.13
  11.8 1.6 copy.40
  13.4 0.0 copy-start.9
  13.4 0.0 copy-start.10
  13.4 0.0 copy-start.6
  13.4 0.0 copy-start.7
  13.4 0.0 copy-start.8
  13.5 1.9 copy.39
  15.3 0.0 copy-done.2
  15.3 1.2 copy.41
  16.5 0.0 copy-done.9
  16.5 0.0 copy-done.10
  16.5 0.6 fusion.12.vec
  17.1 0.0 copy-done.6
  17.1 0.0 copy-done.7
  17.1 0.0 copy-done.8
  17.1 0.8 pad_maximum_fusion.1.s_small
  17.9 1.0 fusion.3
  18.9 0.9 pad_maximum_fusion.tables
  19.9 0.6 broadcast_in_dim.61.text_bias
  20.5 0.6 broadcast_in_dim.58.key_bias
  21.1 145.5 %forward.1 = (bf16[1536,1152]{1,0:T(8,128)(2,1)}, bf16[1536,1152]{1,0:T(8,128)(2,1)}, bf16[1536,1536]{1,0:T(8,128)(2,1)}, bf16[1536,3072]{1,0:T(8,128)(2,1)}, f3...) custom-call(bf16[512,1536]{1,0:T(8,128)(2,1)} %tokens.3, ...), custom_call_target="tpu_custom_call" | custom-call | tf_op jit(solution)/shard_map/forward/pallas_call | solution.py:618
  166.6 205.5 %backward.1 = (bf16[512,1536]{1,0:T(8,128)(2,1)}, bf16[512,1536]{1,0:T(8,128)(2,1)}, f32[8,1536]{1,0:T(8,128)}, bf16[1536,1536]{1,0:T(8,128)(2,1)}, bf16[1536,30...) custom-call(bf16[512,1536]{1,0:T(8,128)(2,1)} %tokens.3, ...), custom_call_target="tpu_custom_call" | custom-call | tf_op jit(solution)/shard_map/backward/pallas_call | solution.py:1155
  372.2 2.0 copy.33
  374.1 0.0 reduce-scatter.4.cloned.1.call-update
  374.1 103.7 %scatter_all.1 = (f32[192,1536]{1,0:T(8,128)}, f32[192,3072]{1,0:T(8,128)}, f32[192,1152]{1,0:T(8,128)}, f32[96,768]{1,0:T(8,128)}, f32[192,1152]{1,0:T(8,128)}) custom-call(bf16[4,2,192,1536]{3,2,1,0:T(8,128)(2,1)} %bitcast.31, bf16[4,2,192,3072]{3,2,1,0:T(8,128)(2,1)} %bitcast.29, bf16[4,2,192,1152]{3,2,1,0:T(8,128)(2,1)} %bitcast.32, ...), custom_call_target="tpu_custom_call" | custom-call | tf_op jit(solution)/shard_map/scatter_all/pallas_call | solution.py:1276
  477.8 0.0 copy-start.1
  477.8 2.2 slice_bitcast_fusion
  480.0 0.0 copy-done.1
  480.0 0.0 copy-start.4
  480.0 0.0 copy-start.5
  480.0 2.1 convert_element_type.21
  482.1 0.0 copy-start
  482.1 0.0 copy-done.4
  482.1 1.0 copy.43
  483.1 0.0 copy-done.5
  483.1 0.9 reshape.306
  484.0 0.1 copy-done
  484.1 3.0 reshape.307
  487.1 0.0 reduce-scatter.4.cloned.1.call-done
  487.1 1.0 slice.25
  488.1 1.0 slice.26
  489.1 1.0 copy.35
  490.1 8.9 %psum.7 = f32[3,192]{1,0:T(4,128)} all-reduce(f32[3,192]{1,0:T(4,128)S(1)} %copy.35), channel_id=1, replica_groups=mesh['dp'=8,'mp'=4] {'mp'}, use_global_device_ids=true, to_apply=%region_1.2 | all-reduce | flops 576 | bytes 4608 | tf_op jit(solution)/shard_map/psum | solution.py:1739
  499.0 0.7 copy.36
  499.7 0.6 copy.37
  500.3 0.0 copy-start.3
  500.3 2.7 copy.46
  503.0 0.0 copy-done.3
  503.0 1.0 copy.47
  (4 shorter events, 0.0 us)
Async XLA Ops:
  7.2 8.2 %copy-start.2 = (bf16[192,2,1536]{2,1,0:T(2,128)(2,1)S(1)}, bf16[192,2,1536]{2,1,0:T(2,128)(2,1)}, u32[]{:S(2)}) copy-start(bf16[192,2,1536]{2,1,0:T(2,128)(2,1)} %param.24) | copy-start | bytes 3538948
  7.2 479.9 %reduce-scatter.4.cloned.1.call-start = ((), (), s32[]{:S(2)}) async-start(), calls=%async_computation.1 | async-start | bytes 884736
  13.4 3.1 copy-start.9
  13.4 3.1 copy-start.10
  13.4 3.7 copy-start.6
  13.4 3.7 copy-start.7
  13.4 3.7 copy-start.8
  477.8 2.2 copy-start.1
  480.0 2.1 copy-start.4
  480.0 3.0 copy-start.5
  482.1 2.0 copy-start
  500.3 2.8 copy-start.3
Sparse Core Ops, SparseCore 0:
  374.3 42.5 reduce-scatter.3
